TPU v7x, 256 devices: a whole 4x4x8 slice. The times are simulated.
256 devices in a mesh: sec: 16 (over x_hi, y, core), tile: 16 (over x_lo, z).
Axes of the slice: x: 4 (x_hi: 2, x_lo: 2; x = x_hi * 2 + x_lo), y: 4, z: 8, core: 2. Of those that a mesh axis runs over, the one named last changes fastest.
Arguments:
- sections: float32 [16, 2, 256, 2560], P('sec', None, None, 'tile'), may hold values from -6 to 6
- prior: float32 [2, 256, 2560], P(None, None, 'tile'), may hold values from -6 to 6
Outputs:
- peak_maps: float32 [16, 2, 1, 64, 256, 256], P('sec', None, None, 'tile')
All inputs are finite; a program needn't handle non-finite values.
Results may differ from a plain program's by a relative error of at most 0.0097.
Values may be sent and summed in bfloat16 or wider, within the bound.
A program may use at most 64 MiB of HBM per device.

v0:
```python
import math

import jax
import jax.numpy as jnp
from jax import lax
from jax.sharding import PartitionSpec as P

PATCH = 256
STRIDE = 40
PC = 4
HALO = 108


eps = 1e-06


def padded(block, sides, width):
    for axis, dim in sides:
        count = lax.axis_size(axis)
        forward = [(i, i + 1) for i in range(count - 1)]
        backward = [(target, source) for source, target in forward]
        low = lax.ppermute(
            lax.slice_in_dim(block, block.shape[dim] - width, None, axis=dim), axis, forward
        )
        high = lax.ppermute(lax.slice_in_dim(block, 0, width, axis=dim), axis, backward)
        block = jnp.concatenate([low, block, high], axis=dim)
    return block


def from_behind(value, axis, steps):
    count = lax.axis_size(axis)
    leading, last = (max(0, -steps), min(count, count - steps))
    return lax.ppermute(value, axis, [(source, source + steps) for source in range(leading, last)])


def tables():
    index = jnp.arange(PATCH, dtype=jnp.int32)
    product = index[:, None] * index[None, :] % PATCH
    angle = product.astype(jnp.float32) * (2.0 * math.pi / PATCH)
    return (jnp.cos(angle).astype(jnp.bfloat16), jnp.sin(angle).astype(jnp.bfloat16))


def cut_patches(wide):
    starts = jnp.arange(PC, dtype=jnp.int32) * STRIDE
    pieces = jax.vmap(lambda begin: lax.dynamic_slice_in_dim(wide, begin, PATCH, 2))(starts)
    bands = [jnp.transpose(pieces, (1, 0, 2, 3))]
    return jnp.stack(bands, axis=1)


def spectra(patches, cosine, sine):
    centered = patches - jnp.mean(patches, axis=(-2, -1), keepdims=True)
    lowered = centered.astype(jnp.bfloat16)
    right = jnp.concatenate([cosine, -sine], axis=1)
    rowed = jnp.einsum(
        "...mn,nk->...mk", lowered, right, preferred_element_type=jnp.float32
    ).astype(jnp.bfloat16)
    first = jnp.einsum("km,...mq->...kq", cosine, rowed, preferred_element_type=jnp.float32)
    second = jnp.einsum("km,...mq->...kq", sine, rowed, preferred_element_type=jnp.float32)
    real = first[..., :PATCH] + second[..., PATCH:]
    imag = first[..., PATCH:] - second[..., :PATCH]
    return jnp.concatenate([real, imag], axis=-1).astype(jnp.bfloat16)


def energies(spectrum):
    values = spectrum.astype(jnp.float32)
    return jnp.sum(values * values, axis=(-2, -1)) / (PATCH * PATCH)


def peaks(spec_now, spec_prev, cosine, sine):
    now = spec_now.astype(jnp.float32)
    prev = spec_prev.astype(jnp.float32)
    now_re, now_im = (now[..., :PATCH], now[..., PATCH:])
    prev_re, prev_im = (prev[..., :PATCH], prev[..., PATCH:])
    cross_re = now_re * prev_re + now_im * prev_im
    cross_im = now_im * prev_re - now_re * prev_im
    cross = jnp.concatenate([cross_re, cross_im], axis=-1).astype(jnp.bfloat16)
    first = jnp.einsum("km,...mq->...kq", cosine, cross, preferred_element_type=jnp.float32)
    second = jnp.einsum("km,...mq->...kq", sine, cross, preferred_element_type=jnp.float32)
    turned_re = first[..., :PATCH] - second[..., PATCH:]
    turned_im = second[..., :PATCH] + first[..., PATCH:]
    turned = jnp.concatenate([turned_re, turned_im], axis=-1).astype(jnp.bfloat16)
    left = jnp.concatenate([cosine, -sine], axis=0)
    real = jnp.einsum("...mq,qn->...mn", turned, left, preferred_element_type=jnp.float32)
    scale = PATCH * jnp.sqrt(energies(spec_now) + eps) * jnp.sqrt(energies(spec_prev) + eps)
    return real / scale[..., None, None]


def local(sections, prior):
    cosine, sine = tables()
    both = jnp.stack([sections[0], prior])
    widened = padded(both, (("tile", 3),), HALO)
    wide_own = widened[0]
    wide_prior = widened[1]
    first_section = lax.axis_index("sec") == 0
    spec_now = spectra(cut_patches(wide_own), cosine, sine)
    arrived = from_behind(spec_now, "sec", 1)
    spec_prev = lax.cond(
        first_section, lambda: spectra(cut_patches(wide_prior), cosine, sine), lambda: arrived
    )
    result = peaks(spec_now, spec_prev, cosine, sine)
    return result[None]


def solution(mesh):
    return jax.shard_map(
        local,
        mesh=mesh,
        in_specs=(P("sec", None, None, "tile"), P(None, None, "tile")),
        out_specs=P("sec", None, None, "tile", None, None),
        check_vma=False,
    )
```

profile of v0, /device:TPU:102, one launch (start us, length us, event | category | flops | bytes accessed | tf_op | source)
XLA Modules:
  0.0 92.3 jit_solution(17554259563292918448)
XLA Ops:
  0.0 1.2 %copy.42 = f32[1,2,256,160]{2,1,3,0:T(2,128)S(1)} copy(f32[1,2,256,160]{2,3,1,0:T(8,128)} %param.4) | data formatting | bytes 655360 | tf_op args[0]
  1.2 1.2 %copy.72 = f32[2,256,160]{1,0,2:T(2,128)S(1)} copy(f32[2,256,160]{1,2,0:T(8,128)} %param.5) | data formatting | bytes 655360 | tf_op args[1]
  2.5 0.4 fusion.30
  2.9 5.0 %collective-permute-start = (f32[2,2,256,108]{2,1,3,0:T(2,128)S(1)}, f32[2,2,256,108]{2,1,3,0:T(2,128)S(1)}, u32[]{:S(2)}, u32[]{:S(2)}) collective-permute-start(f32[2,2,256,108]{2,1,3,0:T(2,128)S(1)} %get-tuple-element.106), channel_id=1, source_target_pairs={{0,1},{1,2},{2,3},{3,4},{4,5},{5,6},{6,7},{7,8},{8,9},{9,10},{10,1... | collective-permute-start | bytes 1327112 | tf_op jit(solution)/shard_map/ppermute | solution.py:22
  7.9 1.9 %collective-permute-start.1 = (f32[2,2,256,108]{2,1,3,0:T(2,128)S(1)}, f32[2,2,256,108]{2,1,3,0:T(2,128)S(1)}, u32[]{:S(2)}, u32[]{:S(2)}) collective-permute-start(f32[2,2,256,108]{2,1,3,0:T(2,128)S(1)} %get-tuple-element.107), channel_id=1, source_target_pairs={{1,0},{2,1},{3,2},{4,3},{5,4},{6,5},{7,6},{8,7},{9,8},{10,9},{11,1... | collective-permute-start | bytes 1327112 | tf_op jit(solution)/shard_map/ppermute | solution.py:25
  9.9 1.0 %cosine_convert_fusion = bf16[256,256]{1,0:T(8,128)(2,1)S(1)} fusion(), kind=kLoop, calls=%fused_computation.79 | loop fusion | flops 983040 | bytes 131072 | tf_op jit(solution)/shard_map/convert_element_type | solution.py:40
  10.8 1.0 %fusion.45 = bf16[256,256]{1,0:T(8,128)(2,1)S(1)} fusion(), kind=kLoop, calls=%fused_computation.87 | loop fusion | flops 1179648 | bytes 131072 | tf_op jit(solution)/shard_map/neg | solution.py:53
  11.8 5.5 %collective-permute-done = f32[2,2,256,108]{2,1,3,0:T(2,128)S(1)} collective-permute-done((f32[2,2,256,108]{2,1,3,0:T(2,128)S(1)}, f32[2,2,256,108]{2,1,3,0:T(2,128)S(1)}, u32[]{:S(2)}, u32[]{:S(2)}) %collective-permute-start) | collective-permute-done | bytes 442400 | tf_op jit(solution)/shard_map/ppermute | solution.py:22
  17.3 5.3 %collective-permute-done.1 = f32[2,2,256,108]{2,1,3,0:T(2,128)S(1)} collective-permute-done((f32[2,2,256,108]{2,1,3,0:T(2,128)S(1)}, f32[2,2,256,108]{2,1,3,0:T(2,128)S(1)}, u32[]{:S(2)}, u32[]{:S(2)}) %collective-permute-start.1) | collective-permute-done | bytes 442400 | tf_op jit(solution)/shard_map/ppermute | solution.py:25
  22.6 0.7 pad_maximum_fusion.2
  23.4 0.0 copy-start.1
  23.4 1.1 %copy-done.1 = f32[2,2,256,376]{2,1,3,0:T(2,128)} copy-done((f32[2,2,256,376]{2,1,3,0:T(2,128)}, f32[2,2,256,376]{2,1,3,0:T(2,128)S(1)}, u32[]{:S(2)}) %copy-start.1) | copy-done | bytes 1540120
  24.5 0.3 slice_bitcast_fusion.1
  24.8 4.0 %gather_fusion.1 = f32[4,2,256,256]{2,1,3,0:T(2,128)} fusion(f32[2,256,376]{1,0,2:T(2,128)S(1)} %slice_bitcast_fusion.1, s32[4]{0:T(128)S(1)} %fusion.48), kind=kCustom, calls=%fused_computation.1 | custom fusion | bytes 4194352 | tf_op jit(solution)/shard_map/vmap()/gather | solution.py:45
  28.8 2.7 %copy.43 = f32[4,2,256,256]{3,2,0,1:T(8,128)S(1)} copy(f32[4,2,256,256]{2,1,3,0:T(2,128)} %gather_fusion.1) | data formatting | bytes 4194304 | tf_op jit(solution)/shard_map/vmap()/gather | solution.py:45
  31.5 0.2 bitcast_reduce_fusion.1
  31.7 0.1 copy.70
  31.8 0.1 copy.45
  31.9 0.7 convolution_convert_fusion.1
  32.7 1.7 %convolution_bitcast_fusion.4 = f32[2,1,4,256,512]{3,4,2,0,1:T(8,128)S(1)} fusion(bf16[2,4,256,512]{3,2,1,0:T(8,128)(2,1)S(1)} %convolution_convert_fusion.1), kind=kOutput, calls=%fused_computation.31 | convolution fusion | flops 537853952 | bytes 6291456 | tf_op jit(solution)/shard_map/km,...mq->...kq/dot_general | solution.py:58
  34.4 1.7 %convolution_bitcast_fusion.5 = f32[2,1,4,256,512]{3,4,2,0,1:T(8,128)S(1)} fusion(bf16[2,4,256,512]{3,2,1,0:T(8,128)(2,1)S(1)} %convolution_convert_fusion.1), kind=kOutput, calls=%fused_computation.32 | convolution fusion | flops 537853952 | bytes 6291456 | tf_op jit(solution)/shard_map/km,...mq->...kq/dot_general | solution.py:57
  36.0 1.0 %fusion.16 = (bf16[2,1,4,256,256]{3,4,2,0,1:T(8,128)(2,1)S(1)}, bf16[2,1,4,256,256]{3,4,2,0,1:T(8,128)(2,1)S(1)}) fusion(f32[2,1,4,256,512]{3,4,2,0,1:T(8,128)S(1)} %convolution_bitcast_fusion.4, f32[2,1,4,256,512]{3,4,2,0,1:T(8,128)S(1)} %convolution_bitcast_fusion.5), kind=kLoop, calls=%fused_computation.40 | loop fusion | flops 2097152 | bytes 10485760 | tf_op jit(solution)/shard_map/convert.10
  37.0 0.0 copy-start
  37.0 3.2 %fusion.69 = (f32[2,1,4,256,512]{3,4,2,0,1:T(8,128)}, bf16[2,1,4,256,512]{3,4,2,0,1:T(8,128)(2,1)}) fusion(bf16[2,1,4,256,256]{3,4,2,0,1:T(8,128)(2,1)S(1)} %get-tuple-element.103, bf16[2,1,4,256,256]{3,4,2,0,1:T(8,128)(2,1)S(1)} %get-tuple-element.102), kind=kLoop, calls=%fused_computation.114 | loop fusion | flops 5242880 | bytes 8388608 | tf_op jit(solution)/shard_map/convert_element_type | solution.py:70
  40.2 0.0 copy-done
  40.2 2.1 %collective-permute-start.2 = (bf16[2,1,4,256,512]{3,4,2,0,1:T(8,128)(2,1)}, bf16[2,1,4,256,512]{3,4,2,0,1:T(8,128)(2,1)S(1)}, u32[]{:S(2)}, u32[]{:S(2)}) collective-permute-start(bf16[2,1,4,256,512]{3,4,2,0,1:T(8,128)(2,1)} %get-tuple-element.105), channel_id=1, source_target_pairs={{0,16},{16,32},{32,48},{48,64},{64,80},{80,96},{96,112},{112,128},... | collective-permute-start | bytes 6291464 | tf_op jit(solution)/shard_map/ppermute | solution.py:33
  42.3 1.0 %sine_convert_fusion = bf16[256,256]{1,0:T(8,128)(2,1)S(1)} fusion(), kind=kLoop, calls=%fused_computation.78 | loop fusion | flops 983040 | bytes 131072 | tf_op jit(solution)/shard_map/convert_element_type | solution.py:40
  43.3 1.8 %multiply_reduce_fusion.2 = f32[2,4]{1,0:T(2,128)S(1)} fusion(bf16[2,1,4,256,256]{3,4,2,0,1:T(8,128)(2,1)} %copy-done, bf16[2,1,4,256,256]{3,4,2,0,1:T(8,128)(2,1)S(1)} %get-tuple-element.102), kind=kLoop, calls=%fused_computation.28 | loop fusion | flops 6291448 | bytes 2097184 | tf_op jit(solution)/shard_map/reduce_sum | solution.py:66
  45.1 0.1 copy.49
  45.2 26.2 %collective-permute-done.2 = bf16[2,1,4,256,512]{3,4,2,0,1:T(8,128)(2,1)S(1)} collective-permute-done((bf16[2,1,4,256,512]{3,4,2,0,1:T(8,128)(2,1)}, bf16[2,1,4,256,512]{3,4,2,0,1:T(8,128)(2,1)S(1)}, u32[]{:S(2)}, u32[]{:S(2)}) %collective-permute-start.2) | collective-permute-done | bytes 2097184 | tf_op jit(solution)/shard_map/ppermute | solution.py:33
  71.4 3.1 %conditional.1 = (f32[2,1,4,256,256]{3,4,2,0,1:T(8,128)}, f32[2,1,4,256,256]{3,4,2,0,1:T(8,128)}, f32[2,4]{0,1:T(4,128)S(1)}) conditional(s32[]{:T(128)} %convert_element_type.159, bf16[2,1,4,256,512]{3,4,2,0,1:T(8,128)(2,1)S(1)} %collective-permute-done.2, (f32[2,2,256,376]{2,1,3,0:T(2,128)}, bf16[256,256]{1,0:T(8,128)(2,1)S(1)}, ...), branch_computations={%region_1.3_spmd.clone.clone, %region_3.6_spmd.clone.clone} | conditional | flops 1626406912 | bytes 56852792 | solution.py:97
  71.4 0.6 multiply_reduce_fusion
  72.0 0.1 copy.67
  72.1 2.5 %fusion.70 = (f32[2,1,4,256,256]{3,4,2,0,1:T(8,128)}, f32[2,1,4,256,256]{3,4,2,0,1:T(8,128)}) fusion(bf16[2,1,4,256,512]{3,4,2,0,1:T(8,128)(2,1)S(1)} %param.8), kind=kLoop, calls=%fused_computation.115 | loop fusion | bytes 8388608 | tf_op jit(solution)/shard_map/slice | solution.py:73
  74.5 4.2 %fusion.24 = (bf16[2,4,256,256]{2,3,1,0:T(8,128)(2,1)S(1)}, bf16[2,4,256,256]{2,3,1,0:T(8,128)(2,1)S(1)}) fusion(f32[2,1,4,256,256]{3,4,2,0,1:T(8,128)} %get-tuple-element.78, f32[2,1,4,256,512]{3,4,2,0,1:T(8,128)} %get-tuple-element.104, f32[2,1,4,256,256]{3,4,2,0,1:T(8,128)} %get-tuple-element.79), kind=kLoop, calls=%fused_computation.55 | loop fusion | flops 4194304 | bytes 10485760 | tf_op jit(solution)/shard_map/concatenate | solution.py:76
  78.8 3.6 %convolution_bitcast_fusion.2 = f32[2,1,4,256,512]{3,4,2,0,1:T(8,128)} fusion(bf16[2,4,256,256]{2,3,1,0:T(8,128)(2,1)S(1)} %get-tuple-element.101, bf16[2,4,256,256]{2,3,1,0:T(8,128)(2,1)S(1)} %get-tuple-element.100), kind=kOutput, calls=%fused_computation.29 | convolution fusion | flops 542048256 | bytes 6291456 | tf_op jit(solution)/shard_map/km,...mq->...kq/dot_general | solution.py:78
  82.3 3.6 %convolution_bitcast_fusion.3 = f32[2,1,4,256,512]{3,4,2,0,1:T(8,128)} fusion(bf16[2,4,256,256]{2,3,1,0:T(8,128)(2,1)S(1)} %get-tuple-element.101, bf16[2,4,256,256]{2,3,1,0:T(8,128)(2,1)S(1)} %get-tuple-element.100), kind=kOutput, calls=%fused_computation.30 | convolution fusion | flops 542048256 | bytes 6291456 | tf_op jit(solution)/shard_map/km,...mq->...kq/dot_general | solution.py:77
  86.0 0.1 copy.51
  86.1 4.1 %fusion.27 = (bf16[2,4,256,256]{2,3,1,0:T(8,128)(2,1)S(1)}, bf16[2,4,256,256]{2,3,1,0:T(8,128)(2,1)S(1)}) fusion(f32[2,1,4,256,512]{3,4,2,0,1:T(8,128)} %convolution_bitcast_fusion.2, f32[2,1,4,256,512]{3,4,2,0,1:T(8,128)} %convolution_bitcast_fusion.3), kind=kLoop, calls=%fused_computation.57 | loop fusion | flops 2097152 | bytes 10485760 | tf_op jit(solution)/shard_map/concatenate | solution.py:81
  90.2 2.1 %divide_bitcast_fusion = f32[1,2,1,4,256,256]{5,4,3,2,1,0:T(8,128)} fusion(bf16[2,4,256,256]{2,3,1,0:T(8,128)(2,1)S(1)} %get-tuple-element.99, bf16[2,4,256,256]{2,3,1,0:T(8,128)(2,1)S(1)} %get-tuple-element.98, f32[2,4]{1,0:T(2,128)S(1)} %copy.51, bf16[256,256]{1,0:T(8,128)(2,1)S(1)} %fusion.45, bf16[256,256]{1,0:T(8,128)(2,1)S(1)} %cosine_convert_fusion), kind=kOutput, calls=%fused_computation.50 | convolution fusion | flops 542113792 | bytes 4456480 | tf_op jit(solution)/shard_map/...mq,qn->...mn/dot_general | solution.py:83
  (3 shorter events, 0.0 us)
Async XLA Ops:
  2.9 14.4 %collective-permute-start = (f32[2,2,256,108]{2,1,3,0:T(2,128)S(1)}, f32[2,2,256,108]{2,1,3,0:T(2,128)S(1)}, u32[]{:S(2)}, u32[]{:S(2)}) collective-permute-start(f32[2,2,256,108]{2,1,3,0:T(2,128)S(1)} %get-tuple-element.106), channel_id=1, source_target_pairs={{0,1},{1,2},{2,3},{3,4},{4,5},{5,6},{6,7},{7,8},{8,9},{9,10},{10,1... | collective-permute-start | bytes 1327112 | tf_op jit(solution)/shard_map/ppermute | solution.py:22
  7.9 14.7 %collective-permute-start.1 = (f32[2,2,256,108]{2,1,3,0:T(2,128)S(1)}, f32[2,2,256,108]{2,1,3,0:T(2,128)S(1)}, u32[]{:S(2)}, u32[]{:S(2)}) collective-permute-start(f32[2,2,256,108]{2,1,3,0:T(2,128)S(1)} %get-tuple-element.107), channel_id=1, source_target_pairs={{1,0},{2,1},{3,2},{4,3},{5,4},{6,5},{7,6},{8,7},{9,8},{10,9},{11,1... | collective-permute-start | bytes 1327112 | tf_op jit(solution)/shard_map/ppermute | solution.py:25
  23.4 1.1 %copy-start.1 = (f32[2,2,256,376]{2,1,3,0:T(2,128)}, f32[2,2,256,376]{2,1,3,0:T(2,128)S(1)}, u32[]{:S(2)}) copy-start(f32[2,2,256,376]{2,1,3,0:T(2,128)S(1)} %pad_maximum_fusion.2) | copy-start | bytes 4620292
  37.0 3.2 %copy-start = (bf16[2,1,4,256,256]{3,4,2,0,1:T(8,128)(2,1)}, bf16[2,1,4,256,256]{3,4,2,0,1:T(8,128)(2,1)S(1)}, u32[]{:S(2)}) copy-start(bf16[2,1,4,256,256]{3,4,2,0,1:T(8,128)(2,1)S(1)} %get-tuple-element.103) | copy-start | bytes 3145732
  40.2 31.2 %collective-permute-start.2 = (bf16[2,1,4,256,512]{3,4,2,0,1:T(8,128)(2,1)}, bf16[2,1,4,256,512]{3,4,2,0,1:T(8,128)(2,1)S(1)}, u32[]{:S(2)}, u32[]{:S(2)}) collective-permute-start(bf16[2,1,4,256,512]{3,4,2,0,1:T(8,128)(2,1)} %get-tuple-element.105), channel_id=1, source_target_pairs={{0,16},{16,32},{32,48},{48,64},{64,80},{80,96},{96,112},{112,128},... | collective-permute-start | bytes 6291464 | tf_op jit(solution)/shard_map/ppermute | solution.py:33
where the time goes:
time: 92.7 us; the launch traced here: 92.3 us
  waiting for transfers between devices  37 us (40%)
  other arithmetic  19.2 us (21%)
  local copies, waits for them, and re-layouts  13.5 us (15%)
  matrix products  13.4 us (14%)
  starting transfers between devices  9.05 us (10%)
    ppermute x1, waiting for transfers between devices, from_behind(): lax.ppermute(value, axis, [(source, source + steps) for source in range(l...  26.2 us
    gather x2, local copies, waits for them, and re-layouts, cut_patches(): lax.dynamic_slice_in_dim(wide, begin, PATCH, 2)  6.73 us
    ppermute x1, waiting for transfers between devices, padded(): lax.ppermute(lax.slice_in_dim(block, block.shape[dim] - width, None, axis...  5.48 us
    ppermute x1, waiting for transfers between devices, padded(): lax.ppermute(lax.slice_in_dim(block, 0, width, axis=dim), axis, backward)  5.33 us
    ppermute x1, starting transfers between devices, padded(): lax.ppermute(lax.slice_in_dim(block, block.shape[dim] - width, None, axis...  5.04 us
    concatenate x1, other arithmetic, peaks(): cross = jnp.concatenate([cross_re, cross_im], axis=-1).astype(jnp.bfloat16)  4.22 us
    concatenate x1, other arithmetic, peaks(): jnp.concatenate([turned_re, turned_im], axis=-1).astype(jnp.bfloat16)  4.14 us
    unnamed x7, local copies, waits for them, and re-layouts  3.69 us
  transfers between devices with their start and end apart: 3, of which 3 were waited for; matrix products, arithmetic and copies ran while one was open for 5% of the time, Pallas kernels for 0%

commit v1 on v0

v1 whole, which is shorter than its diff:
```python
import functools

import jax
import jax.numpy as jnp
import ml_dtypes
import numpy as np
from jax import lax
from jax.experimental import pallas as pl
from jax.experimental.pallas import tpu as pltpu
from jax.sharding import PartitionSpec as P

N = 256
H = 128
STRIDE = 40
PC = 4
HALO = 108
LEVELS = 2
COLS = 160
EDGE = 112
EPS = 1e-06
MESH = pl.DeviceIdType.MESH
f32, bf16 = jnp.float32, jnp.bfloat16


def tables():
    i = np.arange(N)
    product = i[:, None] * i[None, :] % N
    cos = np.cos(product * (2.0 * np.pi / N))
    sin = np.sin(product * (2.0 * np.pi / N))
    alternate = cos[:, H]
    columns = np.concatenate([cos[:, :H], -sin[:, :H]], axis=1)
    columns[:, 0] = 0.0
    columns[:, H] = alternate
    ahead = np.concatenate([cos[:H], sin[:H]], axis=0)
    ahead[H] = alternate
    back = 2.0 * np.concatenate([cos[:, :H], sin[:, :H]], axis=1)
    back[:, 0] = 1.0
    back[:, H] = alternate
    last = 2.0 * np.concatenate([cos[:, :H], -sin[:, :H]], axis=1)
    last[:, 0] = alternate
    last[:, H] = 0.0
    lowered = [a.astype(ml_dtypes.bfloat16) for a in (columns, ahead, back, cos, sin)]
    return np.stack(lowered), last.astype(ml_dtypes.bfloat16)


def dot(a, b):
    return jnp.dot(a, b, preferred_element_type=f32)


def column_stage(x, table):
    mean = jnp.sum(x, axis=1, keepdims=True) * (1.0 / N)
    low = x - mean
    energy = jnp.sum(low * low, axis=1, keepdims=True)
    return dot(low.astype(bf16), table).astype(bf16), mean, energy


def side_rows(means, energies):
    lane = lax.broadcasted_iota(jnp.int32, (COLS, H), 1)
    block = jnp.zeros((COLS, H), f32)
    for at, value in enumerate(means + energies):
        block = jnp.where(lane == at, value, block)
    block = jnp.concatenate([block, jnp.zeros((N - COLS, H), f32)], axis=0)
    return jnp.transpose(block)[:8]


def windows(own, left, right, at):
    row = lax.broadcasted_iota(jnp.int32, (8, N), 0)
    lane = lax.broadcasted_iota(jnp.int32, (8, N), 1)
    patch = row % PC
    begin = patch * STRIDE + (N - HALO)
    from_left = (patch < PC - 1) & (lane >= begin)
    from_right = (lane >= COLS) | ((patch == PC - 1) & (lane < begin - N))

    def spread(side):
        return jnp.where(row < PC, side[at : at + 1], side[at + 1 : at + 2])

    return jnp.where(from_left, spread(left), jnp.where(from_right, spread(right), spread(own)))


def centre(own, left, right, at):
    means = windows(own, left, right, at)
    means = means - jnp.sum(means, axis=1, keepdims=True) * (1.0 / N)
    energies = windows(own, left, right, at + 2) + N * means * means
    return jnp.concatenate([N * means, energies], axis=0)


def mixed(upper, lower, split):
    row = lax.broadcasted_iota(jnp.int32, upper.shape, 0)
    return jnp.where(row < split, upper.astype(f32), lower.astype(f32)).astype(bf16)


def patch_of(j, level, own, left, right):
    if j == 0:
        parts = [
            own[level, 0:144],
            mixed(own[level, 144:160], left[level, 0:16], 4),
            left[level, 16:112],
        ]
    elif j == 1:
        parts = [
            own[level, 0:160],
            right[level, 0:16],
            mixed(right[level, 16:32], left[level, 32:48], 12),
            left[level, 48:112],
        ]
    elif j == 2:
        parts = [
            own[level, 0:160],
            right[level, 0:64],
            mixed(right[level, 64:80], left[level, 80:96], 4),
            left[level, 96:112],
        ]
    else:
        parts = [
            mixed(right[level, 96:112], own[level, 0:16], 12),
            own[level, 16:160],
            right[level, 0:96],
        ]
    return jnp.concatenate(parts, axis=0)


def cross(now, prev, out):
    step = 16
    for begin in range(0, H, step):
        even, odd = pl.ds(begin, step), pl.ds(H + begin, step)
        a_er, a_ei, a_oi, a_or = now[even, :H], now[even, H:], now[odd, :H], now[odd, H:]
        b_er, b_ei, b_oi, b_or = prev[even, :H], prev[even, H:], prev[odd, :H], prev[odd, H:]
        ee_r = a_er * b_er + a_ei * b_ei
        ee_i = a_ei * b_er - a_er * b_ei
        oo_r = a_or * b_or + a_oi * b_oi
        oo_i = a_or * b_oi - a_oi * b_or
        odd_r = (a_er * b_or - a_ei * b_oi) + (a_or * b_er - a_oi * b_ei)
        minus_i = (a_oi * b_er + a_or * b_ei) - (a_ei * b_or + a_er * b_oi)
        if begin == 0:
            first = lax.broadcasted_iota(jnp.int32, (step, H), 0) == 0
            even_r = jnp.where(first, ee_r, ee_r + oo_r)
            even_i = jnp.where(first, ee_i, ee_i + oo_i)
            minus_i = jnp.where(first, oo_r, minus_i)
            odd_r = jnp.where(first, oo_i, odd_r)
        else:
            even_r, even_i = ee_r + oo_r, ee_i + oo_i
        out[even, :H] = even_r.astype(bf16)
        out[even, H:] = even_i.astype(bf16)
        out[odd, :H] = minus_i.astype(bf16)
        out[odd, H:] = odd_r.astype(bf16)


def first_kernel(
    n_sec,
    n_tile,
    x_hbm,
    prior_hbm,
    table_hbm,
    turned,
    rows_out,
    x,
    prior,
    table,
    a_own,
    a_left,
    a_right,
    b_own,
    b_left,
    b_right,
    side,
    side_out,
    side_in,
    a_rows,
    b_rows,
    spec_a,
    spec_b,
    crossed,
    load_sem,
    send_sem,
    recv_sem,
):
    s, t = lax.axis_index("sec"), lax.axis_index("tile")
    has_left, has_right = t > 0, t < n_tile - 1
    has_next, has_prev = s < n_sec - 1, s > 0
    even = s % 2 == 0
    to_left, to_right, to_next = {"tile": t - 1}, {"tile": t + 1}, {"sec": s + 1}

    def load(source, target, at):
        return pltpu.make_async_copy(source, target, load_sem.at[at])

    load_x = [load(x_hbm.at[i], x.at[i], i) for i in range(LEVELS)]
    load_first = load(table_hbm.at[0], table.at[0], 2)
    load_rest = load(table_hbm.at[1:5], table.at[1:5], 3)
    load_prior = load(prior_hbm, prior, 4)
    load_first.start()
    for copy in load_x:
        copy.start()
    load_rest.start()

    barrier = pltpu.get_barrier_semaphore()

    def greet(there, device):
        @pl.when(there)
        def _():
            pl.semaphore_signal(barrier, inc=1, device_id=device, device_id_type=MESH)

    greet(has_left, to_left)
    greet(has_right, to_right)
    greet(has_prev, {"sec": s - 1})

    @pl.when(s == 0)
    def _():
        load_prior.start()

    started = []
    count = [0]

    def remote(source, target, device, arrival):
        at = count[0]
        count[0] += 1
        return pltpu.make_async_remote_copy(
            src_ref=source,
            dst_ref=target,
            send_sem=send_sem.at[at],
            recv_sem=recv_sem.at[arrival],
            device_id=device,
            device_id_type=MESH,
        )

    def send(there, *what):
        copy = remote(*what)
        pl.when(there)(copy.start)
        started.append((there, copy))

    def arrived(there, target, arrival):
        copy = pltpu.make_async_remote_copy(
            src_ref=target,
            dst_ref=target,
            send_sem=send_sem.at[0],
            recv_sem=recv_sem.at[arrival],
            device_id=to_next,
            device_id_type=MESH,
        )
        if there is None:
            copy.wait_recv()
        else:
            pl.when(there)(copy.wait_recv)

    @pl.when(jnp.logical_not(has_left))
    def _():
        a_left[...] = jnp.zeros_like(a_left)
        b_left[...] = jnp.zeros_like(b_left)
        side_in[0] = jnp.zeros((8, N), f32)

    @pl.when(jnp.logical_not(has_right))
    def _():
        a_right[...] = jnp.zeros_like(a_right)
        b_right[...] = jnp.zeros_like(b_right)
        side_in[1] = jnp.zeros((8, N), f32)

    low, high = pl.ds(0, EDGE), pl.ds(COLS - EDGE, EDGE)
    load_first.wait()
    means, energies = [], []
    for i in range(LEVELS):
        load_x[i].wait()
        spectrum, mean, energy = column_stage(x[i], table[0])
        a_own[i] = spectrum
        means.append(mean)
        energies.append(energy)
        if i == 0:
            neighbours = [has_left, has_right, has_next]
            pl.semaphore_wait(barrier, sum(v.astype(jnp.int32) for v in neighbours))
        send(has_right, a_own.at[i, high], a_left.at[i], to_right, i)
        send(has_left, a_own.at[i, low], a_right.at[i], to_left, 2 + i)
        send(has_next, a_own.at[i], b_own.at[i], to_next, 4 + i)

    side[...] = side_rows(means, energies)

    @pl.when(s == 0)
    def _():
        load_prior.wait()
        prior_means, prior_energies = [], []
        for i in range(LEVELS):
            spectrum, mean, energy = column_stage(prior[i], table[0])
            b_own[i] = spectrum
            prior_means.append(mean)
            prior_energies.append(energy)
        rows = side_rows(prior_means, prior_energies)
        side[4:8] = rows[0:4]

    side_out[0] = pltpu.roll(side[...], N - COLS, 1)
    side_out[1] = pltpu.roll(side[...], COLS, 1)
    send(has_right, side_out.at[0], side_in.at[0], to_right, 10)
    send(has_left, side_out.at[1], side_in.at[1], to_left, 11)

    for i in range(LEVELS):
        arrived(has_left, a_left.at[i], i)
        arrived(has_right, a_right.at[i], 2 + i)
        forward = even & has_next
        send(forward & has_left, a_left.at[i], b_left.at[i], to_next, 6 + i)
        send(forward & has_right, a_right.at[i], b_right.at[i], to_next, 8 + i)
        arrived(has_prev, b_own.at[i], 4 + i)
        send(even & has_right, b_own.at[i, high], b_left.at[i], to_right, 6 + i)
        send(even & has_left, b_own.at[i, low], b_right.at[i], to_left, 8 + i)

    load_rest.wait()
    arrived(has_left, side_in.at[0], 10)
    arrived(has_right, side_in.at[1], 11)
    a_rows[...] = centre(side[...], side_in[0], side_in[1], 0)
    send(has_next, a_rows, b_rows, to_next, 12)

    @pl.when(s == 0)
    def _():
        b_rows[...] = centre(side[...], side_in[0], side_in[1], 4)

    arrived(has_prev, b_rows, 12)
    pair = jnp.concatenate([a_rows[0:8], b_rows[0:8]], axis=0).astype(bf16)
    even_part, odd_part = dot(pair, table[3]), dot(pair, table[4])
    a_e, b_e, a_o, b_o = even_part[:8], even_part[8:], odd_part[:8], odd_part[8:]
    both = jnp.concatenate([a_e * b_e + a_o * b_o, a_e * b_o - a_o * b_e], axis=0).astype(bf16)
    flat = dot(both, table[3])[:8] - dot(both, table[4])[8:]
    energy_a = jnp.sum(a_rows[8:16], axis=1, keepdims=True)
    energy_b = jnp.sum(b_rows[8:16], axis=1, keepdims=True)
    scale = 1.0 / (N * jnp.sqrt(energy_a + EPS) * jnp.sqrt(energy_b + EPS))
    rows_out[0:8] = flat * scale
    rows_out[8:16] = jnp.broadcast_to(scale, (8, N))

    @pl.loop(0, LEVELS)
    def _(i):
        for there, target, arrival in (
            (has_left, b_left, 6),
            (has_right, b_right, 8),
        ):
            arrived(there, target.at[i], arrival + i)
        for j in range(PC):
            spec_a[...] = dot(table[1], patch_of(j, i, a_own, a_left, a_right))
            spec_b[...] = dot(table[1], patch_of(j, i, b_own, b_left, b_right))
            cross(spec_a, spec_b, crossed)
            turned[i * PC + j] = dot(table[2], crossed[...]).astype(bf16)

    for there, copy in started:
        pl.when(there)(copy.wait_send)


def last_kernel(turned, rows, table, out_hbm, held, sem):
    copies = []
    for p in range(LEVELS * PC):
        product = lax.dot_general(
            table[...], turned[p], (((1,), (1,)), ((), ())), preferred_element_type=f32
        )
        held[p] = product * rows[8 + p : 9 + p] + rows[p : p + 1]
        copy = pltpu.make_async_copy(held.at[p], out_hbm.at[p], sem.at[p])
        copy.start()
        copies.append(copy)
    for copy in copies:
        copy.wait()


def local(n_sec, n_tile, sections, prior):
    x = jnp.swapaxes(sections[0], 1, 2)
    before = jnp.swapaxes(prior, 1, 2)
    table, last = tables()
    anywhere = pl.BlockSpec(memory_space=pl.ANY)
    vmem = pl.BlockSpec(memory_space=pltpu.VMEM)
    patches = LEVELS * PC
    half = lambda rows: pltpu.VMEM((LEVELS, rows, N), bf16)
    turned, rows = pl.pallas_call(
        functools.partial(first_kernel, n_sec, n_tile),
        out_shape=(
            jax.ShapeDtypeStruct((patches, N, N), bf16),
            jax.ShapeDtypeStruct((16, N), f32),
        ),
        in_specs=[anywhere] * 3,
        out_specs=(vmem, vmem),
        scratch_shapes=[
            pltpu.VMEM((LEVELS, COLS, N), f32),
            pltpu.VMEM((LEVELS, COLS, N), f32),
            pltpu.VMEM((5, N, N), bf16),
            half(COLS),
            half(EDGE),
            half(EDGE),
            half(COLS),
            half(EDGE),
            half(EDGE),
            pltpu.VMEM((8, N), f32),
            pltpu.VMEM((2, 8, N), f32),
            pltpu.VMEM((2, 8, N), f32),
            pltpu.VMEM((16, N), f32),
            pltpu.VMEM((16, N), f32),
            pltpu.VMEM((N, N), f32),
            pltpu.VMEM((N, N), f32),
            pltpu.VMEM((N, N), bf16),
            pltpu.SemaphoreType.DMA((5,)),
            pltpu.SemaphoreType.DMA((17,)),
            pltpu.SemaphoreType.DMA((13,)),
        ],
        compiler_params=pltpu.CompilerParams(
            collective_id=0, has_side_effects=True, vmem_limit_bytes=16 * 2**20
        ),
        name="spectra",
    )(x, before, jnp.asarray(table))
    maps = pl.pallas_call(
        last_kernel,
        out_shape=jax.ShapeDtypeStruct((patches, N, N), f32),
        in_specs=[vmem] * 3,
        out_specs=anywhere,
        scratch_shapes=[pltpu.VMEM((patches, N, N), f32), pltpu.SemaphoreType.DMA((patches,))],
        compiler_params=pltpu.CompilerParams(vmem_limit_bytes=16 * 2**20),
        name="maps",
    )(turned, rows, jnp.asarray(last))
    return maps.reshape(1, LEVELS, 1, PC, N, N)


def solution(mesh):
    return jax.shard_map(
        functools.partial(local, mesh.shape["sec"], mesh.shape["tile"]),
        mesh=mesh,
        in_specs=(P("sec", None, None, "tile"), P(None, None, "tile")),
        out_specs=P("sec", None, None, "tile", None, None),
        check_vma=False,
    )
```

time: 92.7 us -> 25.6 us (0.28)
  the two profiles are of different devices: /device:TPU:102 before, /device:TPU:6 now
where the time goes in v1:
time: 25.6 us; the launch traced here: 25.3 us
  Pallas kernels  21.4 us (84%)
  local copies, waits for them, and re-layouts  3.93 us (15%)
    pallas_call x1, Pallas kernels, local(): pl.pallas_call(functools.partial(first_kernel, n_sec, n_tile), out_shape=...  19.8 us
    unnamed x8, local copies, waits for them, and re-layouts  3.93 us
    pallas_call x1, Pallas kernels, local(): pl.pallas_call(last_kernel, out_shape=jax.ShapeDtypeStruct((patches, N, N...  1.64 us

profile of v1, /device:TPU:6, one launch (start us, length us, event | category | flops | bytes accessed | tf_op | source)
XLA Modules:
  0.0 25.3 jit_solution(1938411364642077015)
XLA Ops:
  0.0 0.0 copy-start
  0.0 1.1 %copy-done = bf16[5,256,256]{2,1,0:T(8,128)(2,1)S(1)} copy-done((bf16[5,256,256]{2,1,0:T(8,128)(2,1)S(1)}, bf16[5,256,256]{2,1,0:T(8,128)(2,1)}, u32[]{:S(2)}) %copy-start) | copy-done | bytes 655384
  1.1 0.0 copy-start.1
  1.1 1.0 %copy-done.1 = f32[1,2,256,160]{2,3,1,0:T(8,128)S(1)} copy-done((f32[1,2,256,160]{2,3,1,0:T(8,128)S(1)}, f32[1,2,256,160]{2,3,1,0:T(8,128)}, u32[]{:S(2)}) %copy-start.1) | copy-done | bytes 327704
  2.1 0.0 copy-start.2
  2.1 1.0 %copy-done.2 = f32[2,256,160]{1,2,0:T(8,128)S(1)} copy-done((f32[2,256,160]{1,2,0:T(8,128)S(1)}, f32[2,256,160]{1,2,0:T(8,128)}, u32[]{:S(2)}) %copy-start.2) | copy-done | bytes 327704
  3.0 19.8 %spectra.1 = (bf16[8,256,256]{2,1,0:T(8,128)(2,1)S(1)}, f32[16,256]{1,0:T(8,128)S(1)}) custom-call(f32[2,160,256]{2,1,0:T(8,128)S(1)} %bitcast.7, f32[2,160,256]{2,1,0:T(8,128)S(1)} %bitcast.8, bf16[5,256,256]{2,1,0:T(8,128)(2,1)S(1)} %copy-done), custom_call_target="tpu_custom_call" | custom-call | tf_op jit(solution)/shard_map/spectra/pallas_call | solution.py:362
  22.8 0.0 copy-start.3
  22.8 0.9 %copy-done.3 = bf16[256,256]{1,0:T(8,128)(2,1)S(1)} copy-done((bf16[256,256]{1,0:T(8,128)(2,1)S(1)}, bf16[256,256]{1,0:T(8,128)(2,1)}, u32[]{:S(2)}) %copy-start.3) | copy-done | bytes 131096
  23.7 1.6 %maps.1 = f32[8,256,256]{2,1,0:T(8,128)} custom-call(bf16[8,256,256]{2,1,0:T(8,128)(2,1)S(1)} %get-tuple-element.7.turned, f32[16,256]{1,0:T(8,128)S(1)} %get-tuple-element.8.rows, bf16[256,256]{1,0:T(8,128)(2,1)S(1)} %copy-done.3), custom_call_target="tpu_custom_call" | custom-call | tf_op jit(solution)/shard_map/maps/pallas_call | solution.py:397
Async XLA Ops:
  0.0 1.1 %copy-start = (bf16[5,256,256]{2,1,0:T(8,128)(2,1)S(1)}, bf16[5,256,256]{2,1,0:T(8,128)(2,1)}, u32[]{:S(2)}) copy-start(bf16[5,256,256]{2,1,0:T(8,128)(2,1)} %constant.4.clone.table_hbm) | copy-start | bytes 1966084
  1.1 1.0 %copy-start.1 = (f32[1,2,256,160]{2,3,1,0:T(8,128)S(1)}, f32[1,2,256,160]{2,3,1,0:T(8,128)}, u32[]{:S(2)}) copy-start(f32[1,2,256,160]{2,3,1,0:T(8,128)} %param.4) | copy-start | bytes 983044
  2.1 1.0 %copy-start.2 = (f32[2,256,160]{1,2,0:T(8,128)S(1)}, f32[2,256,160]{1,2,0:T(8,128)}, u32[]{:S(2)}) copy-start(f32[2,256,160]{1,2,0:T(8,128)} %param.5) | copy-start | bytes 983044
  22.8 0.9 %copy-start.3 = (bf16[256,256]{1,0:T(8,128)(2,1)S(1)}, bf16[256,256]{1,0:T(8,128)(2,1)}, u32[]{:S(2)}) copy-start(bf16[256,256]{1,0:T(8,128)(2,1)} %constant.5.clone.table) | copy-start | bytes 393220

commit v2 on v1

--- a/solution.py
+++ b/solution.py
@@ -39,8 +39,8 @@
     last = 2.0 * np.concatenate([cos[:, :H], -sin[:, :H]], axis=1)
     last[:, 0] = alternate
     last[:, H] = 0.0
-    lowered = [a.astype(ml_dtypes.bfloat16) for a in (columns, ahead, back, cos, sin)]
-    return np.stack(lowered), last.astype(ml_dtypes.bfloat16)
+    lowered = [a.astype(ml_dtypes.bfloat16) for a in (columns, ahead, back, cos, sin, last)]
+    return np.stack(lowered)
 
 
 def dot(a, b):
@@ -77,11 +77,11 @@
     return jnp.where(from_left, spread(left), jnp.where(from_right, spread(right), spread(own)))
 
 
-def centre(own, left, right, at):
-    means = windows(own, left, right, at)
+def centre(own, left, right):
+    means = windows(own, left, right, 0)
     means = means - jnp.sum(means, axis=1, keepdims=True) * (1.0 / N)
-    energies = windows(own, left, right, at + 2) + N * means * means
-    return jnp.concatenate([N * means, energies], axis=0)
+    energies = windows(own, left, right, 2) + N * means * means
+    return N * means, jnp.sum(energies, axis=1, keepdims=True)
 
 
 def mixed(upper, lower, split):
@@ -153,20 +153,20 @@
     table_hbm,
     turned,
     rows_out,
+    table,
+    spec_later,
+    b_own,
+    b_left,
+    b_right,
     x,
     prior,
-    table,
     a_own,
     a_left,
     a_right,
-    b_own,
-    b_left,
-    b_right,
     side,
     side_out,
     side_in,
-    a_rows,
-    b_rows,
+    b_side,
     spec_a,
     spec_b,
     crossed,
@@ -177,7 +177,10 @@
     s, t = lax.axis_index("sec"), lax.axis_index("tile")
     has_left, has_right = t > 0, t < n_tile - 1
     has_next, has_prev = s < n_sec - 1, s > 0
-    even = s % 2 == 0
+    middle = n_tile // 2
+    direct_out = (t == middle - 1) & (s % 2 == 1) & has_next & (s != n_sec // 2 - 1)
+    direct_in = (t == middle) & (s % 2 == 0) & has_prev & (s != n_sec // 2)
+    direct_past = (t == middle) & (s % 2 == 1) & has_next & (s != n_sec // 2 - 1)
     to_left, to_right, to_next = {"tile": t - 1}, {"tile": t + 1}, {"sec": s + 1}
 
     def load(source, target, at):
@@ -185,7 +188,7 @@
 
     load_x = [load(x_hbm.at[i], x.at[i], i) for i in range(LEVELS)]
     load_first = load(table_hbm.at[0], table.at[0], 2)
-    load_rest = load(table_hbm.at[1:5], table.at[1:5], 3)
+    load_rest = load(table_hbm.at[1:6], table.at[1:6], 3)
     load_prior = load(prior_hbm, prior, 4)
     load_first.start()
     for copy in load_x:
@@ -202,6 +205,7 @@
     greet(has_left, to_left)
     greet(has_right, to_right)
     greet(has_prev, {"sec": s - 1})
+    greet(direct_in, {"sec": s - 1, "tile": t - 1})
 
     @pl.when(s == 0)
     def _():
@@ -246,107 +250,132 @@
         a_left[...] = jnp.zeros_like(a_left)
         b_left[...] = jnp.zeros_like(b_left)
         side_in[0] = jnp.zeros((8, N), f32)
+        b_side[1] = jnp.zeros((8, N), f32)
 
     @pl.when(jnp.logical_not(has_right))
     def _():
         a_right[...] = jnp.zeros_like(a_right)
         b_right[...] = jnp.zeros_like(b_right)
         side_in[1] = jnp.zeros((8, N), f32)
+        b_side[2] = jnp.zeros((8, N), f32)
 
     low, high = pl.ds(0, EDGE), pl.ds(COLS - EDGE, EDGE)
+    to_direct = {"sec": s + 1, "tile": t + 1}
+
+    def send_columns(i):
+        send(has_right, a_own.at[i, high], a_left.at[i], to_right, i)
+        send(direct_out, a_own.at[i, high], b_left.at[i], to_direct, 6 + i)
+        send(has_left, a_own.at[i, low], a_right.at[i], to_left, 2 + i)
+        send(has_next, a_own.at[i], b_own.at[i], to_next, 4 + i)
+
     load_first.wait()
-    means, energies = [], []
+    stats = []
     for i in range(LEVELS):
         load_x[i].wait()
-        spectrum, mean, energy = column_stage(x[i], table[0])
-        a_own[i] = spectrum
-        means.append(mean)
-        energies.append(energy)
+        a_own[i], *stat = column_stage(x[i], table[0])
+        stats.append(stat)
         if i == 0:
-            neighbours = [has_left, has_right, has_next]
-            pl.semaphore_wait(barrier, sum(v.astype(jnp.int32) for v in neighbours))
-        send(has_right, a_own.at[i, high], a_left.at[i], to_right, i)
-        send(has_left, a_own.at[i, low], a_right.at[i], to_left, 2 + i)
-        send(has_next, a_own.at[i], b_own.at[i], to_next, 4 + i)
-
-    side[...] = side_rows(means, energies)
+            targets = [has_left, has_right, has_next, direct_out]
+            pl.semaphore_wait(barrier, sum(v.astype(jnp.int32) for v in targets))
+            send_columns(i)
+    side[...] = side_rows(*zip(*stats))
 
     @pl.when(s == 0)
     def _():
         load_prior.wait()
-        prior_means, prior_energies = [], []
+        prior_stats = []
         for i in range(LEVELS):
-            spectrum, mean, energy = column_stage(prior[i], table[0])
-            b_own[i] = spectrum
-            prior_means.append(mean)
-            prior_energies.append(energy)
-        rows = side_rows(prior_means, prior_energies)
+            b_own[i], *stat = column_stage(prior[i], table[0])
+            prior_stats.append(stat)
+        rows = side_rows(*zip(*prior_stats))
         side[4:8] = rows[0:4]
 
     side_out[0] = pltpu.roll(side[...], N - COLS, 1)
     side_out[1] = pltpu.roll(side[...], COLS, 1)
     send(has_right, side_out.at[0], side_in.at[0], to_right, 10)
+    send(direct_out, side_out.at[0], b_side.at[1], to_direct, 13)
     send(has_left, side_out.at[1], side_in.at[1], to_left, 11)
-
+    send(has_next, side, b_side.at[0], to_next, 12)
+    send_columns(LEVELS - 1)
     for i in range(LEVELS):
+        send((s == 0) & has_right, b_own.at[i, high], b_left.at[i], to_right, 6 + i)
+        send((s == 0) & has_left, b_own.at[i, low], b_right.at[i], to_left, 8 + i)
+
+    passed_on = has_next & has_left & jnp.logical_not(direct_past)
+    for i in range(LEVELS):
+        arrived(has_right, a_right.at[i], 2 + i)
+        send(has_next & has_right, a_right.at[i], b_right.at[i], to_next, 8 + i)
         arrived(has_left, a_left.at[i], i)
-        arrived(has_right, a_right.at[i], 2 + i)
-        forward = even & has_next
-        send(forward & has_left, a_left.at[i], b_left.at[i], to_next, 6 + i)
-        send(forward & has_right, a_right.at[i], b_right.at[i], to_next, 8 + i)
+        send(passed_on, a_left.at[i], b_left.at[i], to_next, 6 + i)
+        if i == 0:
+            arrived(has_right, side_in.at[1], 11)
+            send(has_next & has_right, side_in.at[1], b_side.at[2], to_next, 14)
+            arrived(has_left, side_in.at[0], 10)
+            send(passed_on, side_in.at[0], b_side.at[1], to_next, 13)
+
+    load_rest.wait()
+    for j in range(PC):
+        spec_a[j] = dot(table[1], patch_of(j, 0, a_own, a_left, a_right))
+    for j in range(PC):
+        spec_later[j] = dot(table[1], patch_of(j, 1, a_own, a_left, a_right))
+
+    def previous_arrived(i):
         arrived(has_prev, b_own.at[i], 4 + i)
-        send(even & has_right, b_own.at[i, high], b_left.at[i], to_right, 6 + i)
-        send(even & has_left, b_own.at[i, low], b_right.at[i], to_left, 8 + i)
-
-    load_rest.wait()
-    arrived(has_left, side_in.at[0], 10)
-    arrived(has_right, side_in.at[1], 11)
-    a_rows[...] = centre(side[...], side_in[0], side_in[1], 0)
-    send(has_next, a_rows, b_rows, to_next, 12)
+        arrived(has_right, b_right.at[i], 8 + i)
+        arrived(has_left, b_left.at[i], 6 + i)
+
+    previous_arrived(0)
+    for j in range(PC):
+        spec_b[j] = dot(table[1], patch_of(j, 0, b_own, b_left, b_right))
+    for j in range(PC):
+        cross(spec_a.at[j], spec_b.at[j], crossed.at[j])
+        turned[j] = dot(table[2], crossed[j]).astype(bf16)
+
+    arrived(has_prev, b_side.at[0], 12)
+    arrived(has_prev & has_right, b_side.at[2], 14)
+    arrived(has_prev & has_left, b_side.at[1], 13)
 
     @pl.when(s == 0)
     def _():
-        b_rows[...] = centre(side[...], side_in[0], side_in[1], 4)
-
-    arrived(has_prev, b_rows, 12)
-    pair = jnp.concatenate([a_rows[0:8], b_rows[0:8]], axis=0).astype(bf16)
+        b_side[0] = pltpu.roll(side[...], 4, 0)
+        b_side[1] = pltpu.roll(side_in[0], 4, 0)
+        b_side[2] = pltpu.roll(side_in[1], 4, 0)
+
+    a_flat, a_energy = centre(side[...], side_in[0], side_in[1])
+    b_flat, b_energy = centre(b_side[0], b_side[1], b_side[2])
+    pair = jnp.concatenate([a_flat, b_flat], axis=0).astype(bf16)
     even_part, odd_part = dot(pair, table[3]), dot(pair, table[4])
     a_e, b_e, a_o, b_o = even_part[:8], even_part[8:], odd_part[:8], odd_part[8:]
     both = jnp.concatenate([a_e * b_e + a_o * b_o, a_e * b_o - a_o * b_e], axis=0).astype(bf16)
     flat = dot(both, table[3])[:8] - dot(both, table[4])[8:]
-    energy_a = jnp.sum(a_rows[8:16], axis=1, keepdims=True)
-    energy_b = jnp.sum(b_rows[8:16], axis=1, keepdims=True)
-    scale = 1.0 / (N * jnp.sqrt(energy_a + EPS) * jnp.sqrt(energy_b + EPS))
+    scale = 1.0 / (N * jnp.sqrt(a_energy + EPS) * jnp.sqrt(b_energy + EPS))
     rows_out[0:8] = flat * scale
     rows_out[8:16] = jnp.broadcast_to(scale, (8, N))
 
-    @pl.loop(0, LEVELS)
-    def _(i):
-        for there, target, arrival in (
-            (has_left, b_left, 6),
-            (has_right, b_right, 8),
-        ):
-            arrived(there, target.at[i], arrival + i)
-        for j in range(PC):
-            spec_a[...] = dot(table[1], patch_of(j, i, a_own, a_left, a_right))
-            spec_b[...] = dot(table[1], patch_of(j, i, b_own, b_left, b_right))
-            cross(spec_a, spec_b, crossed)
-            turned[i * PC + j] = dot(table[2], crossed[...]).astype(bf16)
-
+    previous_arrived(1)
     for there, copy in started:
         pl.when(there)(copy.wait_send)
 
 
-def last_kernel(turned, rows, table, out_hbm, held, sem):
+def last_kernel(turned, rows, table, spec_a, b_own, b_left, b_right, out_hbm, spec_b, crossed, held, sem):
     copies = []
-    for p in range(LEVELS * PC):
+
+    def finish(p, turned_p):
         product = lax.dot_general(
-            table[...], turned[p], (((1,), (1,)), ((), ())), preferred_element_type=f32
+            table[5], turned_p, (((1,), (1,)), ((), ())), preferred_element_type=f32
         )
         held[p] = product * rows[8 + p : 9 + p] + rows[p : p + 1]
         copy = pltpu.make_async_copy(held.at[p], out_hbm.at[p], sem.at[p])
         copy.start()
         copies.append(copy)
+
+    for j in range(PC):
+        finish(j, turned[j])
+    for j in range(PC):
+        spec_b[j] = dot(table[1], patch_of(j, 1, b_own, b_left, b_right))
+    for j in range(PC):
+        cross(spec_a.at[j], spec_b.at[j], crossed.at[j])
+        finish(PC + j, dot(table[2], crossed[j]).astype(bf16))
     for copy in copies:
         copy.wait()
 
@@ -354,55 +383,61 @@
 def local(n_sec, n_tile, sections, prior):
     x = jnp.swapaxes(sections[0], 1, 2)
     before = jnp.swapaxes(prior, 1, 2)
-    table, last = tables()
-    anywhere = pl.BlockSpec(memory_space=pl.ANY)
+    hbm = pl.BlockSpec(memory_space=pltpu.HBM)
     vmem = pl.BlockSpec(memory_space=pltpu.VMEM)
     patches = LEVELS * PC
-    half = lambda rows: pltpu.VMEM((LEVELS, rows, N), bf16)
-    turned, rows = pl.pallas_call(
+    columns = lambda rows: pltpu.VMEM((LEVELS, rows, N), bf16)
+    held = lambda *shape: jax.ShapeDtypeStruct(shape, bf16)
+    operands = (x, before, jnp.asarray(tables()))
+    results = pl.pallas_call(
         functools.partial(first_kernel, n_sec, n_tile),
         out_shape=(
-            jax.ShapeDtypeStruct((patches, N, N), bf16),
+            held(PC, N, N),
             jax.ShapeDtypeStruct((16, N), f32),
+            held(6, N, N),
+            jax.ShapeDtypeStruct((PC, N, N), f32),
+            held(LEVELS, COLS, N),
+            held(LEVELS, EDGE, N),
+            held(LEVELS, EDGE, N),
         ),
-        in_specs=[anywhere] * 3,
-        out_specs=(vmem, vmem),
+        in_specs=[hbm] * 3,
+        out_specs=(vmem,) * 7,
         scratch_shapes=[
             pltpu.VMEM((LEVELS, COLS, N), f32),
             pltpu.VMEM((LEVELS, COLS, N), f32),
-            pltpu.VMEM((5, N, N), bf16),
-            half(COLS),
-            half(EDGE),
-            half(EDGE),
-            half(COLS),
-            half(EDGE),
-            half(EDGE),
+            columns(COLS),
+            columns(EDGE),
+            columns(EDGE),
             pltpu.VMEM((8, N), f32),
             pltpu.VMEM((2, 8, N), f32),
             pltpu.VMEM((2, 8, N), f32),
-            pltpu.VMEM((16, N), f32),
-            pltpu.VMEM((16, N), f32),
-            pltpu.VMEM((N, N), f32),
-            pltpu.VMEM((N, N), f32),
-            pltpu.VMEM((N, N), bf16),
+            pltpu.VMEM((3, 8, N), f32),
+            pltpu.VMEM((PC, N, N), f32),
+            pltpu.VMEM((PC, N, N), f32),
+            pltpu.VMEM((PC, N, N), bf16),
             pltpu.SemaphoreType.DMA((5,)),
-            pltpu.SemaphoreType.DMA((17,)),
-            pltpu.SemaphoreType.DMA((13,)),
+            pltpu.SemaphoreType.DMA((24,)),
+            pltpu.SemaphoreType.DMA((15,)),
         ],
         compiler_params=pltpu.CompilerParams(
             collective_id=0, has_side_effects=True, vmem_limit_bytes=16 * 2**20
         ),
         name="spectra",
-    )(x, before, jnp.asarray(table))
+    )(*(pltpu.with_memory_space_constraint(v, pltpu.HBM) for v in operands))
     maps = pl.pallas_call(
         last_kernel,
         out_shape=jax.ShapeDtypeStruct((patches, N, N), f32),
-        in_specs=[vmem] * 3,
-        out_specs=anywhere,
-        scratch_shapes=[pltpu.VMEM((patches, N, N), f32), pltpu.SemaphoreType.DMA((patches,))],
+        in_specs=[vmem] * 7,
+        out_specs=hbm,
+        scratch_shapes=[
+            pltpu.VMEM((PC, N, N), f32),
+            pltpu.VMEM((PC, N, N), bf16),
+            pltpu.VMEM((patches, N, N), f32),
+            pltpu.SemaphoreType.DMA((patches,)),
+        ],
         compiler_params=pltpu.CompilerParams(vmem_limit_bytes=16 * 2**20),
         name="maps",
-    )(turned, rows, jnp.asarray(last))
+    )(*results)
     return maps.reshape(1, LEVELS, 1, PC, N, N)
 
 

time: 25.6 us -> 19.9 us (0.78)
  local copies, waits for them, and re-layouts: 3.93 us -> 0 us
  Pallas kernels: 21.4 us -> 19.8 us
    unnamed x8 -> x0, local copies, waits for them, and re-layouts: 3.93 us -> none
    pallas_call x1, Pallas kernels: 19.8 us -> 17.8 us  [local(): pl.pallas_call(functools.partial(first_kernel, n_sec, n_tile), out_shape=...]
    pallas_call x1, Pallas kernels: 1.64 us -> 2 us  [local(): pl.pallas_call(last_kernel, out_shape=jax.ShapeDtypeStruct((patches, N, N...]
where the time goes in v2:
time: 19.9 us; the launch traced here: 19.8 us
  Pallas kernels  19.8 us (99%)
    pallas_call x1, Pallas kernels, local(): pl.pallas_call(functools.partial(first_kernel, n_sec, n_tile), out_shape=...  17.8 us
    pallas_call x1, Pallas kernels, local(): pl.pallas_call(last_kernel, out_shape=jax.ShapeDtypeStruct((patches, N, N...  2 us

profile of v2, /device:TPU:6, one launch (start us, length us, event | category | flops | bytes accessed | tf_op | source)
XLA Modules:
  0.0 19.8 jit_solution(2310744809219347584)
XLA Ops:
  0.0 17.8 %spectra.1 = (bf16[4,256,256]{2,1,0:T(8,128)(2,1)S(1)}, f32[16,256]{1,0:T(8,128)S(1)}, bf16[6,256,256]{2,1,0:T(8,128)(2,1)S(1)}, f32[4,256,256]{2,1,0:T(8,128)S(...) custom-call(f32[2,160,256]{2,1,0:T(8,128)} %bitcast.7, ...), custom_call_target="tpu_custom_call" | custom-call | tf_op jit(solution)/shard_map/spectra/pallas_call | solution.py:392
  17.8 2.0 %maps.1 = f32[8,256,256]{2,1,0:T(8,128)} custom-call(bf16[4,256,256]{2,1,0:T(8,128)(2,1)S(1)} %get-tuple-element.12.turned, f32[16,256]{1,0:T(8,128)S(1)} %get-tuple-element.13.rows, bf16[6,256,256]{2,1,0:T(8,128)(2,1)S(1)} %get-tuple-element.14.table, f32[4,256,256]{2,1,0:T(8,128)S(1)} %get-tuple-element.15.spec_a, ...), custom_call_target="tpu_custom_call" | custom-call | tf_op jit(solution)/shard_map/maps/pallas_call | solution.py:427

commit v3 on v2

--- a/solution.py
+++ b/solution.py
@@ -151,7 +151,7 @@
     x_hbm,
     prior_hbm,
     table_hbm,
-    turned,
+    held,
     rows_out,
     table,
     spec_later,
@@ -168,19 +168,32 @@
     side_in,
     b_side,
     spec_a,
+    spec_last,
     spec_b,
     crossed,
+    turned,
+    rows,
     load_sem,
     send_sem,
     recv_sem,
+    ready_sem,
 ):
     s, t = lax.axis_index("sec"), lax.axis_index("tile")
     has_left, has_right = t > 0, t < n_tile - 1
     has_next, has_prev = s < n_sec - 1, s > 0
     middle = n_tile // 2
-    direct_out = (t == middle - 1) & (s % 2 == 1) & has_next & (s != n_sec // 2 - 1)
-    direct_in = (t == middle) & (s % 2 == 0) & has_prev & (s != n_sec // 2)
-    direct_past = (t == middle) & (s % 2 == 1) & has_next & (s != n_sec // 2 - 1)
+    at_middle, before_middle = t == middle, t == middle - 1
+    elsewhere = jnp.logical_not(at_middle)
+    direct_out = (t == middle - 1) & (s % 2 == 1) & has_next
+    direct_in = (t == middle) & (s % 2 == 0) & has_prev
+    direct_past = (t == middle) & (s % 2 == 1) & has_next
+    step = t % middle
+    early, late = at_middle & (s != n_sec // 2), at_middle & (s == n_sec // 2)
+    far, far_next = s == n_sec // 2 - 1, s == n_sec // 2
+    back_out = far & (step >= 1) & (step <= middle // 2)
+    back_in = far_next & (step < middle // 2)
+    back_past = far & (step < middle // 2)
+    late_out, late_in = far & (t == middle - 1), far_next & (t == middle - 1)
     to_left, to_right, to_next = {"tile": t - 1}, {"tile": t + 1}, {"sec": s + 1}
 
     def load(source, target, at):
@@ -203,8 +216,10 @@
             pl.semaphore_signal(barrier, inc=1, device_id=device, device_id_type=MESH)
 
     greet(has_left, to_left)
-    greet(has_right, to_right)
-    greet(has_prev, {"sec": s - 1})
+    greet(has_right & jnp.logical_not(before_middle), to_right)
+    greet(has_prev & jnp.logical_not(late_in), {"sec": s - 1})
+    greet(late_out, to_next)
+    greet(back_in, {"sec": s - 1, "tile": t + 1})
     greet(direct_in, {"sec": s - 1, "tile": t - 1})
 
     @pl.when(s == 0)
@@ -260,13 +275,23 @@
         b_side[2] = jnp.zeros((8, N), f32)
 
     low, high = pl.ds(0, EDGE), pl.ds(COLS - EDGE, EDGE)
-    to_direct = {"sec": s + 1, "tile": t + 1}
+    to_direct, to_back = {"sec": s + 1, "tile": t + 1}, {"sec": s + 1, "tile": t - 1}
+
+    lefts, left_copies = [], {}
+
+    def send_left(what, when):
+        source, target, arrival = what
+        if arrival not in left_copies:
+            left_copies[arrival] = remote(source, target, to_left, arrival)
+            started.append((has_left, left_copies[arrival]))
+        pl.when(when & has_left)(left_copies[arrival].start)
 
     def send_columns(i):
         send(has_right, a_own.at[i, high], a_left.at[i], to_right, i)
         send(direct_out, a_own.at[i, high], b_left.at[i], to_direct, 6 + i)
-        send(has_left, a_own.at[i, low], a_right.at[i], to_left, 2 + i)
-        send(has_next, a_own.at[i], b_own.at[i], to_next, 4 + i)
+        lefts.append((a_own.at[i, low], a_right.at[i], 2 + i))
+        send_left(lefts[-1], elsewhere)
+        send(back_out, a_own.at[i, low], b_right.at[i], to_back, 8 + i)
 
     load_first.wait()
     stats = []
@@ -275,10 +300,48 @@
         a_own[i], *stat = column_stage(x[i], table[0])
         stats.append(stat)
         if i == 0:
-            targets = [has_left, has_right, has_next, direct_out]
-            pl.semaphore_wait(barrier, sum(v.astype(jnp.int32) for v in targets))
+            known = [has_left & elsewhere, has_right, has_next & jnp.logical_not(late_out)]
+            known += [direct_out, back_out, late_in]
+            pl.semaphore_wait(barrier, sum(v.astype(jnp.int32) for v in known))
+
+            @pl.when(before_middle)
+            def _():
+                pl.semaphore_signal(
+                    ready_sem.at[1], inc=1, device_id=to_right, device_id_type=MESH
+                )
+
+            @pl.when(late_in)
+            def _():
+                pl.semaphore_signal(
+                    ready_sem.at[0], inc=1, device_id={"sec": s - 1}, device_id_type=MESH
+                )
+
             send_columns(i)
     side[...] = side_rows(*zip(*stats))
+
+    side_out[0] = pltpu.roll(side[...], N - COLS, 1)
+    side_out[1] = pltpu.roll(side[...], COLS, 1)
+    send(has_right, side_out.at[0], side_in.at[0], to_right, 10)
+    send(direct_out, side_out.at[0], b_side.at[1], to_direct, 13)
+    lefts.append((side_out.at[1], side_in.at[1], 11))
+    send_left(lefts[-1], elsewhere)
+    send(back_out, side_out.at[1], b_side.at[2], to_back, 14)
+    send_columns(LEVELS - 1)
+
+    @pl.when(late_out)
+    def _():
+        pl.semaphore_wait(ready_sem.at[0], 1)
+
+    for i in range(LEVELS):
+        send(has_next, a_own.at[i], b_own.at[i], to_next, 4 + i)
+    send(has_next, side, b_side.at[0], to_next, 12)
+
+    @pl.when(at_middle)
+    def _():
+        pl.semaphore_wait(ready_sem.at[1], 1)
+
+    for what in lefts:
+        send_left(what, at_middle)
 
     @pl.when(s == 0)
     def _():
@@ -287,60 +350,94 @@
         for i in range(LEVELS):
             b_own[i], *stat = column_stage(prior[i], table[0])
             prior_stats.append(stat)
-        rows = side_rows(*zip(*prior_stats))
-        side[4:8] = rows[0:4]
-
-    side_out[0] = pltpu.roll(side[...], N - COLS, 1)
-    side_out[1] = pltpu.roll(side[...], COLS, 1)
-    send(has_right, side_out.at[0], side_in.at[0], to_right, 10)
-    send(direct_out, side_out.at[0], b_side.at[1], to_direct, 13)
-    send(has_left, side_out.at[1], side_in.at[1], to_left, 11)
-    send(has_next, side, b_side.at[0], to_next, 12)
-    send_columns(LEVELS - 1)
+        prior_side = side_rows(*zip(*prior_stats))
+        b_side[0] = prior_side
+        side_out[2] = pltpu.roll(prior_side, N - COLS, 1)
+        side_out[3] = pltpu.roll(prior_side, COLS, 1)
+
+    first_right, first_left = (s == 0) & has_right, (s == 0) & has_left
+    send(first_right, side_out.at[2], b_side.at[1], to_right, 13)
+    send(first_left, side_out.at[3], b_side.at[2], to_left, 14)
     for i in range(LEVELS):
-        send((s == 0) & has_right, b_own.at[i, high], b_left.at[i], to_right, 6 + i)
-        send((s == 0) & has_left, b_own.at[i, low], b_right.at[i], to_left, 8 + i)
-
-    passed_on = has_next & has_left & jnp.logical_not(direct_past)
-    for i in range(LEVELS):
-        arrived(has_right, a_right.at[i], 2 + i)
-        send(has_next & has_right, a_right.at[i], b_right.at[i], to_next, 8 + i)
-        arrived(has_left, a_left.at[i], i)
-        send(passed_on, a_left.at[i], b_left.at[i], to_next, 6 + i)
-        if i == 0:
-            arrived(has_right, side_in.at[1], 11)
-            send(has_next & has_right, side_in.at[1], b_side.at[2], to_next, 14)
-            arrived(has_left, side_in.at[0], 10)
-            send(passed_on, side_in.at[0], b_side.at[1], to_next, 13)
-
-    load_rest.wait()
-    for j in range(PC):
-        spec_a[j] = dot(table[1], patch_of(j, 0, a_own, a_left, a_right))
-    for j in range(PC):
-        spec_later[j] = dot(table[1], patch_of(j, 1, a_own, a_left, a_right))
-
-    def previous_arrived(i):
+        send(first_right, b_own.at[i, high], b_left.at[i], to_right, 6 + i)
+        send(first_left, b_own.at[i, low], b_right.at[i], to_left, 8 + i)
+
+    left_on = has_next & has_left & jnp.logical_not(direct_past)
+    right_on = has_next & has_right & jnp.logical_not(back_past)
+
+    passed = {}
+
+    def pass_on(when, there, on, source, arrival, target, further):
+        arrived(when & there, source, arrival)
+        if arrival not in passed:
+            passed[arrival] = remote(source, target, to_next, further)
+            started.append((on, passed[arrival]))
+        pl.when(when & on)(passed[arrival].start)
+
+    def pass_left(i):
+        pass_on(True, has_left, left_on, a_left.at[i], i, b_left.at[i], 6 + i)
+
+    def pass_right(when, i):
+        pass_on(when, has_right, right_on, a_right.at[i], 2 + i, b_right.at[i], 8 + i)
+
+    def pass_right_side(when):
+        pass_on(when, has_right, right_on, side_in.at[1], 11, b_side.at[2], 14)
+
+    def begin_spectra():
+        for j in range(PC - 1):
+            spec_a[j] = dot(table[1], patch_of(j, 0, a_own, a_left, a_right))
+
+    def previous_right(i):
         arrived(has_prev, b_own.at[i], 4 + i)
         arrived(has_right, b_right.at[i], 8 + i)
-        arrived(has_left, b_left.at[i], 6 + i)
-
-    previous_arrived(0)
-    for j in range(PC):
+
+    def last_patches(*levels):
+        for i in levels:
+            spec_last[i] = dot(table[1], patch_of(PC - 1, i, a_own, a_left, a_right))
+            spec_b[PC - 1 + i] = dot(table[1], patch_of(PC - 1, i, b_own, b_left, b_right))
+        for i in levels:
+            cross(spec_last.at[i], spec_b.at[PC - 1 + i], crossed.at[PC - 1 + i])
+        for i in levels:
+            turned[PC - 1 + i] = dot(table[2], crossed[PC - 1 + i]).astype(bf16)
+
+    upper = step >= middle // 2
+    load_rest.wait()
+    pass_right(at_middle, 0)
+    pass_right(at_middle, 1)
+    pass_right_side(at_middle)
+
+    @pl.when(early)
+    def _():
+        previous_right(0)
+        previous_right(1)
+        last_patches(0, 1)
+
+    pass_left(0)
+    pass_right(upper, 0)
+    pl.when(at_middle)(begin_spectra)
+    pass_on(True, has_left, left_on, side_in.at[0], 10, b_side.at[1], 13)
+    pass_right_side(upper)
+    pass_left(1)
+    pass_right(elsewhere & jnp.logical_not(upper), 0)
+    pass_right(elsewhere, 1)
+    pass_right_side(elsewhere & jnp.logical_not(upper))
+    pl.when(elsewhere)(begin_spectra)
+
+    @pl.when(late)
+    def _():
+        previous_right(0)
+        previous_right(1)
+        last_patches(0, 1)
+
+    pl.when(elsewhere)(lambda: previous_right(0))
+    arrived(has_prev, b_side.at[0], 12)
+    arrived(has_right, b_side.at[2], 14)
+    arrived(has_left, b_side.at[1], 13)
+    arrived(has_left, b_left.at[0], 6)
+    for j in range(PC - 1):
         spec_b[j] = dot(table[1], patch_of(j, 0, b_own, b_left, b_right))
-    for j in range(PC):
-        cross(spec_a.at[j], spec_b.at[j], crossed.at[j])
-        turned[j] = dot(table[2], crossed[j]).astype(bf16)
-
-    arrived(has_prev, b_side.at[0], 12)
-    arrived(has_prev & has_right, b_side.at[2], 14)
-    arrived(has_prev & has_left, b_side.at[1], 13)
-
-    @pl.when(s == 0)
-    def _():
-        b_side[0] = pltpu.roll(side[...], 4, 0)
-        b_side[1] = pltpu.roll(side_in[0], 4, 0)
-        b_side[2] = pltpu.roll(side_in[1], 4, 0)
-
+    for j in range(PC - 1):
+        spec_later[j] = dot(table[1], patch_of(j, 1, a_own, a_left, a_right))
     a_flat, a_energy = centre(side[...], side_in[0], side_in[1])
     b_flat, b_energy = centre(b_side[0], b_side[1], b_side[2])
     pair = jnp.concatenate([a_flat, b_flat], axis=0).astype(bf16)
@@ -349,33 +446,55 @@
     both = jnp.concatenate([a_e * b_e + a_o * b_o, a_e * b_o - a_o * b_e], axis=0).astype(bf16)
     flat = dot(both, table[3])[:8] - dot(both, table[4])[8:]
     scale = 1.0 / (N * jnp.sqrt(a_energy + EPS) * jnp.sqrt(b_energy + EPS))
-    rows_out[0:8] = flat * scale
-    rows_out[8:16] = jnp.broadcast_to(scale, (8, N))
-
-    previous_arrived(1)
+    rows[0:8] = flat * scale
+    rows[8:16] = jnp.broadcast_to(scale, (8, N))
+    for j in range(PC - 1):
+        cross(spec_a.at[j], spec_b.at[j], crossed.at[j])
+    for j in range(PC - 1):
+        turned[j] = dot(table[2], crossed[j]).astype(bf16)
+
+    @pl.when(elsewhere)
+    def _():
+        previous_right(1)
+        last_patches(0, 1)
+
+    for p in range(PC + 1):
+        held[p] = finished(turned[p], table, rows, p if p < PC else 2 * PC - 1)
+    rows_out[...] = rows[...]
     for there, copy in started:
-        pl.when(there)(copy.wait_send)
-
-
-def last_kernel(turned, rows, table, spec_a, b_own, b_left, b_right, out_hbm, spec_b, crossed, held, sem):
+        if copy is not passed[LEVELS - 1]:
+            pl.when(there)(copy.wait_send)
+    arrived(has_left, b_left.at[1], 7)
+    pl.when(left_on)(passed[LEVELS - 1].wait_send)
+
+
+def finished(turned, table, rows, p):
+    product = lax.dot_general(
+        table[5], turned, (((1,), (1,)), ((), ())), preferred_element_type=f32
+    )
+    return product * rows[8 + p : 9 + p] + rows[p : p + 1]
+
+
+def last_kernel(
+    held, rows, table, spec_a, b_own, b_left, b_right, out_hbm, spec_b, crossed, turned, maps, sem
+):
     copies = []
 
-    def finish(p, turned_p):
-        product = lax.dot_general(
-            table[5], turned_p, (((1,), (1,)), ((), ())), preferred_element_type=f32
-        )
-        held[p] = product * rows[8 + p : 9 + p] + rows[p : p + 1]
-        copy = pltpu.make_async_copy(held.at[p], out_hbm.at[p], sem.at[p])
+    def write(source, p):
+        copy = pltpu.make_async_copy(source, out_hbm.at[p], sem.at[p])
         copy.start()
         copies.append(copy)
 
-    for j in range(PC):
-        finish(j, turned[j])
-    for j in range(PC):
+    for p in range(PC + 1):
+        write(held.at[p], p if p < PC else 2 * PC - 1)
+    for j in range(PC - 1):
         spec_b[j] = dot(table[1], patch_of(j, 1, b_own, b_left, b_right))
-    for j in range(PC):
+    for j in range(PC - 1):
         cross(spec_a.at[j], spec_b.at[j], crossed.at[j])
-        finish(PC + j, dot(table[2], crossed[j]).astype(bf16))
+        turned[j] = dot(table[2], crossed[j]).astype(bf16)
+    for j in range(PC - 1):
+        maps[j] = finished(turned[j], table, rows, PC + j)
+        write(maps.at[j], PC + j)
     for copy in copies:
         copy.wait()
 
@@ -392,10 +511,10 @@
     results = pl.pallas_call(
         functools.partial(first_kernel, n_sec, n_tile),
         out_shape=(
-            held(PC, N, N),
+            jax.ShapeDtypeStruct((PC + 1, N, N), f32),
             jax.ShapeDtypeStruct((16, N), f32),
             held(6, N, N),
-            jax.ShapeDtypeStruct((PC, N, N), f32),
+            jax.ShapeDtypeStruct((PC - 1, N, N), f32),
             held(LEVELS, COLS, N),
             held(LEVELS, EDGE, N),
             held(LEVELS, EDGE, N),
@@ -409,15 +528,19 @@
             columns(EDGE),
             columns(EDGE),
             pltpu.VMEM((8, N), f32),
-            pltpu.VMEM((2, 8, N), f32),
+            pltpu.VMEM((4, 8, N), f32),
             pltpu.VMEM((2, 8, N), f32),
             pltpu.VMEM((3, 8, N), f32),
-            pltpu.VMEM((PC, N, N), f32),
-            pltpu.VMEM((PC, N, N), f32),
-            pltpu.VMEM((PC, N, N), bf16),
+            pltpu.VMEM((PC - 1, N, N), f32),
+            pltpu.VMEM((LEVELS, N, N), f32),
+            pltpu.VMEM((PC + 1, N, N), f32),
+            pltpu.VMEM((PC + 1, N, N), bf16),
+            pltpu.VMEM((PC + 1, N, N), bf16),
+            pltpu.VMEM((16, N), f32),
             pltpu.SemaphoreType.DMA((5,)),
-            pltpu.SemaphoreType.DMA((24,)),
+            pltpu.SemaphoreType.DMA((30,)),
             pltpu.SemaphoreType.DMA((15,)),
+            pltpu.SemaphoreType.REGULAR((2,)),
         ],
         compiler_params=pltpu.CompilerParams(
             collective_id=0, has_side_effects=True, vmem_limit_bytes=16 * 2**20
@@ -430,9 +553,10 @@
         in_specs=[vmem] * 7,
         out_specs=hbm,
         scratch_shapes=[
-            pltpu.VMEM((PC, N, N), f32),
-            pltpu.VMEM((PC, N, N), bf16),
-            pltpu.VMEM((patches, N, N), f32),
+            pltpu.VMEM((PC - 1, N, N), f32),
+            pltpu.VMEM((PC - 1, N, N), bf16),
+            pltpu.VMEM((PC - 1, N, N), bf16),
+            pltpu.VMEM((PC - 1, N, N), f32),
             pltpu.SemaphoreType.DMA((patches,)),
         ],
         compiler_params=pltpu.CompilerParams(vmem_limit_bytes=16 * 2**20),

time: 19.9 us -> 16.7 us (0.84)
  the two profiles are of different devices: /device:TPU:6 before, /device:TPU:228 now
where the time goes in v3:
time: 16.7 us; the launch traced here: 16.6 us
  Pallas kernels  16.6 us (99%)
    pallas_call x1, Pallas kernels, local(): pl.pallas_call(functools.partial(first_kernel, n_sec, n_tile), out_shape=...  14.9 us
    pallas_call x1, Pallas kernels, local(): pl.pallas_call(last_kernel, out_shape=jax.ShapeDtypeStruct((patches, N, N...  1.68 us

profile of v3, /device:TPU:228, one launch (start us, length us, event | category | flops | bytes accessed | tf_op | source)
XLA Modules:
  0.0 16.6 jit_solution(14288511460937381048)
XLA Ops:
  0.0 14.9 %spectra.1 = (f32[5,256,256]{2,1,0:T(8,128)S(1)}, f32[16,256]{1,0:T(8,128)S(1)}, bf16[6,256,256]{2,1,0:T(8,128)(2,1)S(1)}, f32[3,256,256]{2,1,0:T(8,128)S(1)}, b...) custom-call(f32[2,160,256]{2,1,0:T(8,128)} %bitcast.7, ...), custom_call_target="tpu_custom_call" | custom-call | tf_op jit(solution)/shard_map/spectra/pallas_call | solution.py:511
  14.9 1.7 %maps.1 = f32[8,256,256]{2,1,0:T(8,128)} custom-call(f32[5,256,256]{2,1,0:T(8,128)S(1)} %get-tuple-element.12.held, f32[16,256]{1,0:T(8,128)S(1)} %get-tuple-element.13.rows, bf16[6,256,256]{2,1,0:T(8,128)(2,1)S(1)} %get-tuple-element.14.table, f32[3,256,256]{2,1,0:T(8,128)S(1)} %get-tuple-element.15.spec_a, ...), custom_call_target="tpu_custom_call" | custom-call | tf_op jit(solution)/shard_map/maps/pallas_call | solution.py:550

commit v4 on v3

--- a/solution.py
+++ b/solution.py
@@ -47,11 +47,10 @@
     return jnp.dot(a, b, preferred_element_type=f32)
 
 
-def column_stage(x, table):
+def column_stats(x):
     mean = jnp.sum(x, axis=1, keepdims=True) * (1.0 / N)
     low = x - mean
-    energy = jnp.sum(low * low, axis=1, keepdims=True)
-    return dot(low.astype(bf16), table).astype(bf16), mean, energy
+    return low.astype(bf16), mean, jnp.sum(low * low, axis=1, keepdims=True)
 
 
 def side_rows(means, energies):
@@ -152,6 +151,7 @@
     prior_hbm,
     table_hbm,
     held,
+    turned_out,
     rows_out,
     table,
     spec_later,
@@ -167,6 +167,8 @@
     side_out,
     side_in,
     b_side,
+    r_own,
+    r_side,
     spec_a,
     spec_last,
     spec_b,
@@ -184,16 +186,21 @@
     middle = n_tile // 2
     at_middle, before_middle = t == middle, t == middle - 1
     elsewhere = jnp.logical_not(at_middle)
-    direct_out = (t == middle - 1) & (s % 2 == 1) & has_next
-    direct_in = (t == middle) & (s % 2 == 0) & has_prev
-    direct_past = (t == middle) & (s % 2 == 1) & has_next
+    crossing = (s % 2 == 1) & has_next
+    left_past = at_middle & crossing
     step = t % middle
-    early, late = at_middle & (s != n_sec // 2), at_middle & (s == n_sec // 2)
+    early = at_middle & (s != n_sec // 2)
+    not_early = jnp.logical_not(early)
     far, far_next = s == n_sec // 2 - 1, s == n_sec // 2
     back_out = far & (step >= 1) & (step <= middle // 2)
     back_in = far_next & (step < middle // 2)
     back_past = far & (step < middle // 2)
-    late_out, late_in = far & (t == middle - 1), far_next & (t == middle - 1)
+    late_out, late_in = far & before_middle, far_next & before_middle
+    relay_out, relay_in = crossing & before_middle, crossing & (t == n_tile - 1)
+    edge_out, edge_in = relay_out & jnp.logical_not(far), relay_in & jnp.logical_not(far)
+    tile_out, tile_in = relay_out & far, relay_in & far
+    not_tile_out = jnp.logical_not(tile_out)
+    first_patches = at_middle & (s % 2 == 0) & has_prev
     to_left, to_right, to_next = {"tile": t - 1}, {"tile": t + 1}, {"sec": s + 1}
 
     def load(source, target, at):
@@ -203,9 +210,9 @@
     load_first = load(table_hbm.at[0], table.at[0], 2)
     load_rest = load(table_hbm.at[1:6], table.at[1:6], 3)
     load_prior = load(prior_hbm, prior, 4)
+    load_x[0].start()
+    load_x[1].start()
     load_first.start()
-    for copy in load_x:
-        copy.start()
     load_rest.start()
 
     barrier = pltpu.get_barrier_semaphore()
@@ -220,14 +227,30 @@
     greet(has_prev & jnp.logical_not(late_in), {"sec": s - 1})
     greet(late_out, to_next)
     greet(back_in, {"sec": s - 1, "tile": t + 1})
-    greet(direct_in, {"sec": s - 1, "tile": t - 1})
+    greet(first_patches & far_next, {"sec": s - 1, "tile": t - 1})
+    greet(relay_in, {"tile": middle - 1})
+    relayed = (first_patches & jnp.logical_not(far_next)) | late_in
+    greet(relayed, {"sec": s - 1, "tile": n_tile - 1})
 
     @pl.when(s == 0)
     def _():
         load_prior.start()
 
-    started = []
+    started = {}
     count = [0]
+
+    def note(there, copy):
+        started.setdefault(id(there), (there, []))[1].append(copy)
+
+    def settle(groups):
+        for there, copies in list(groups.values()):
+
+            @pl.when(there)
+            def _(copies=copies):
+                for copy in copies:
+                    copy.wait_send()
+
+        groups.clear()
 
     def remote(source, target, device, arrival):
         at = count[0]
@@ -244,7 +267,7 @@
     def send(there, *what):
         copy = remote(*what)
         pl.when(there)(copy.start)
-        started.append((there, copy))
+        note(there, copy)
 
     def arrived(there, target, arrival):
         copy = pltpu.make_async_remote_copy(
@@ -276,79 +299,100 @@
 
     low, high = pl.ds(0, EDGE), pl.ds(COLS - EDGE, EDGE)
     to_direct, to_back = {"sec": s + 1, "tile": t + 1}, {"sec": s + 1, "tile": t - 1}
-
-    lefts, left_copies = [], {}
-
-    def send_left(what, when):
-        source, target, arrival = what
-        if arrival not in left_copies:
-            left_copies[arrival] = remote(source, target, to_left, arrival)
-            started.append((has_left, left_copies[arrival]))
-        pl.when(when & has_left)(left_copies[arrival].start)
+    to_last, to_middle = {"tile": n_tile - 1}, {"sec": s + 1, "tile": middle}
+    to_before = {"sec": s + 1, "tile": middle - 1}
+
+    def prepare(there, *what):
+        copy = remote(*what)
+        note(there, copy)
+        return lambda when: pl.when(when & there)(copy.start)
+
+    def columns_to(i):
+        right = prepare(has_right, a_own.at[i, high], a_left.at[i], to_right, i)
+        left = prepare(has_left, a_own.at[i, low], a_right.at[i], to_left, 2 + i)
+        return right, left
 
     def send_columns(i):
-        send(has_right, a_own.at[i, high], a_left.at[i], to_right, i)
-        send(direct_out, a_own.at[i, high], b_left.at[i], to_direct, 6 + i)
-        lefts.append((a_own.at[i, low], a_right.at[i], 2 + i))
-        send_left(lefts[-1], elsewhere)
+        send(tile_out, a_own.at[i, high], b_left.at[i], to_direct, 6 + i)
+        right, left = to_sides[i]
+        right(not_tile_out)
+        send(edge_out, a_own.at[i, high], r_own.at[i, high], to_last, 15 + i)
+        left(elsewhere)
         send(back_out, a_own.at[i, low], b_right.at[i], to_back, 8 + i)
 
-    load_first.wait()
-    stats = []
+    to_sides = [columns_to(i) for i in range(LEVELS)]
+    lowered, stats = [], []
     for i in range(LEVELS):
         load_x[i].wait()
-        a_own[i], *stat = column_stage(x[i], table[0])
+        low_i, *stat = column_stats(x[i])
+        lowered.append(low_i)
         stats.append(stat)
-        if i == 0:
-            known = [has_left & elsewhere, has_right, has_next & jnp.logical_not(late_out)]
-            known += [direct_out, back_out, late_in]
-            pl.semaphore_wait(barrier, sum(v.astype(jnp.int32) for v in known))
-
-            @pl.when(before_middle)
-            def _():
-                pl.semaphore_signal(
-                    ready_sem.at[1], inc=1, device_id=to_right, device_id_type=MESH
-                )
-
-            @pl.when(late_in)
-            def _():
-                pl.semaphore_signal(
-                    ready_sem.at[0], inc=1, device_id={"sec": s - 1}, device_id_type=MESH
-                )
-
-            send_columns(i)
-    side[...] = side_rows(*zip(*stats))
-
-    side_out[0] = pltpu.roll(side[...], N - COLS, 1)
-    side_out[1] = pltpu.roll(side[...], COLS, 1)
+    own_side = side_rows(*zip(*stats))
+    side[...] = own_side
+    side_out[0] = pltpu.roll(own_side, N - COLS, 1)
+    side_out[1] = pltpu.roll(own_side, COLS, 1)
+    load_first.wait()
+    a_own[0] = dot(lowered[0], table[0]).astype(bf16)
+
+    known = [has_left & elsewhere, has_right, has_next & jnp.logical_not(late_out)]
+    known += [relay_out, tile_out, relay_in, back_out, late_in]
+    pl.semaphore_wait(barrier, sum(v.astype(jnp.int32) for v in known))
+
+    @pl.when(before_middle)
+    def _():
+        pl.semaphore_signal(ready_sem.at[1], inc=1, device_id=to_right, device_id_type=MESH)
+
+    @pl.when(late_in)
+    def _():
+        pl.semaphore_signal(
+            ready_sem.at[0], inc=1, device_id={"sec": s - 1}, device_id_type=MESH
+        )
+
     send(has_right, side_out.at[0], side_in.at[0], to_right, 10)
-    send(direct_out, side_out.at[0], b_side.at[1], to_direct, 13)
-    lefts.append((side_out.at[1], side_in.at[1], 11))
-    send_left(lefts[-1], elsewhere)
+    send(tile_out, side_out.at[0], b_side.at[1], to_direct, 13)
+    send(edge_out, side_out.at[0], r_side, to_last, 17)
+    side_left = prepare(has_left, side_out.at[1], side_in.at[1], to_left, 11)
+    side_left(elsewhere)
     send(back_out, side_out.at[1], b_side.at[2], to_back, 14)
-    send_columns(LEVELS - 1)
-
-    @pl.when(late_out)
-    def _():
-        pl.semaphore_wait(ready_sem.at[0], 1)
+    send_columns(0)
+    a_own[1] = dot(lowered[1], table[0]).astype(bf16)
+    send_columns(1)
+    for right, _ in to_sides:
+        right(tile_out)
 
     for i in range(LEVELS):
-        send(has_next, a_own.at[i], b_own.at[i], to_next, 4 + i)
-    send(has_next, side, b_side.at[0], to_next, 12)
+        send(tile_out, a_own.at[i], r_own.at[i], to_last, 15 + i)
+    send(tile_out, side, r_side, to_last, 17)
+    own_on = has_next & not_tile_out
+
+    for i in range(LEVELS):
+        send(own_on, a_own.at[i], b_own.at[i], to_next, 4 + i)
+    send(own_on, side, b_side.at[0], to_next, 12)
+
+    arrived(relay_in, r_side, 17)
+    send(edge_in, r_side, b_side.at[1], to_middle, 13)
+    send(tile_in, r_side, b_side.at[0], to_before, 12)
+    for i in range(LEVELS):
+        arrived(edge_in, r_own.at[i, high], 15 + i)
+        send(edge_in, r_own.at[i, high], b_left.at[i], to_middle, 6 + i)
+        arrived(tile_in, r_own.at[i], 15 + i)
+        send(tile_in, r_own.at[i], b_own.at[i], to_before, 4 + i)
 
     @pl.when(at_middle)
     def _():
         pl.semaphore_wait(ready_sem.at[1], 1)
 
-    for what in lefts:
-        send_left(what, at_middle)
+    side_left(at_middle)
+    for _, left in to_sides:
+        left(at_middle)
 
     @pl.when(s == 0)
     def _():
         load_prior.wait()
         prior_stats = []
         for i in range(LEVELS):
-            b_own[i], *stat = column_stage(prior[i], table[0])
+            low_i, *stat = column_stats(prior[i])
+            b_own[i] = dot(low_i, table[0]).astype(bf16)
             prior_stats.append(stat)
         prior_side = side_rows(*zip(*prior_stats))
         b_side[0] = prior_side
@@ -362,16 +406,23 @@
         send(first_right, b_own.at[i, high], b_left.at[i], to_right, 6 + i)
         send(first_left, b_own.at[i, low], b_right.at[i], to_left, 8 + i)
 
-    left_on = has_next & has_left & jnp.logical_not(direct_past)
+    @pl.when(late_out)
+    def _():
+        pl.semaphore_wait(ready_sem.at[0], 1)
+
+    left_on = has_next & has_left & jnp.logical_not(left_past)
     right_on = has_next & has_right & jnp.logical_not(back_past)
 
     passed = {}
+    last_waits = dict(started)
+    started.clear()
 
     def pass_on(when, there, on, source, arrival, target, further):
         arrived(when & there, source, arrival)
         if arrival not in passed:
             passed[arrival] = remote(source, target, to_next, further)
-            started.append((on, passed[arrival]))
+            if arrival != 1:
+                note(on, passed[arrival])
         pl.when(when & on)(passed[arrival].start)
 
     def pass_left(i):
@@ -412,30 +463,21 @@
         previous_right(1)
         last_patches(0, 1)
 
+    pass_on(True, has_left, left_on, side_in.at[0], 10, b_side.at[1], 13)
+    pass_right_side(upper)
     pass_left(0)
     pass_right(upper, 0)
     pl.when(at_middle)(begin_spectra)
-    pass_on(True, has_left, left_on, side_in.at[0], 10, b_side.at[1], 13)
-    pass_right_side(upper)
     pass_left(1)
     pass_right(elsewhere & jnp.logical_not(upper), 0)
     pass_right(elsewhere, 1)
     pass_right_side(elsewhere & jnp.logical_not(upper))
     pl.when(elsewhere)(begin_spectra)
 
-    @pl.when(late)
-    def _():
-        previous_right(0)
-        previous_right(1)
-        last_patches(0, 1)
-
-    pl.when(elsewhere)(lambda: previous_right(0))
+    settle(last_waits)
     arrived(has_prev, b_side.at[0], 12)
     arrived(has_right, b_side.at[2], 14)
     arrived(has_left, b_side.at[1], 13)
-    arrived(has_left, b_left.at[0], 6)
-    for j in range(PC - 1):
-        spec_b[j] = dot(table[1], patch_of(j, 0, b_own, b_left, b_right))
     for j in range(PC - 1):
         spec_later[j] = dot(table[1], patch_of(j, 1, a_own, a_left, a_right))
     a_flat, a_energy = centre(side[...], side_in[0], side_in[1])
@@ -448,24 +490,29 @@
     scale = 1.0 / (N * jnp.sqrt(a_energy + EPS) * jnp.sqrt(b_energy + EPS))
     rows[0:8] = flat * scale
     rows[8:16] = jnp.broadcast_to(scale, (8, N))
+    rows_out[...] = rows[...]
+
+    pl.when(not_early)(lambda: previous_right(0))
+    arrived(has_left, b_left.at[0], 6)
+    for j in range(PC - 1):
+        spec_b[j] = dot(table[1], patch_of(j, 0, b_own, b_left, b_right))
     for j in range(PC - 1):
         cross(spec_a.at[j], spec_b.at[j], crossed.at[j])
     for j in range(PC - 1):
         turned[j] = dot(table[2], crossed[j]).astype(bf16)
-
-    @pl.when(elsewhere)
+    for j in range(PC - 1):
+        held[j] = finished(turned[j], table, rows, j)
+
+    @pl.when(not_early)
     def _():
         previous_right(1)
         last_patches(0, 1)
 
-    for p in range(PC + 1):
-        held[p] = finished(turned[p], table, rows, p if p < PC else 2 * PC - 1)
-    rows_out[...] = rows[...]
-    for there, copy in started:
-        if copy is not passed[LEVELS - 1]:
-            pl.when(there)(copy.wait_send)
+    for j in range(LEVELS):
+        turned_out[j] = turned[PC - 1 + j]
+    settle(started)
     arrived(has_left, b_left.at[1], 7)
-    pl.when(left_on)(passed[LEVELS - 1].wait_send)
+    pl.when(left_on)(passed[1].wait_send)
 
 
 def finished(turned, table, rows, p):
@@ -476,7 +523,7 @@
 
 
 def last_kernel(
-    held, rows, table, spec_a, b_own, b_left, b_right, out_hbm, spec_b, crossed, turned, maps, sem
+    held, lasts, rows, table, spec_a, b_own, b_left, b_right, out_hbm, spec_b, crossed, turned, maps, sem
 ):
     copies = []
 
@@ -485,10 +532,13 @@
         copy.start()
         copies.append(copy)
 
-    for p in range(PC + 1):
-        write(held.at[p], p if p < PC else 2 * PC - 1)
+    for j in range(PC - 1):
+        write(held.at[j], j)
     for j in range(PC - 1):
         spec_b[j] = dot(table[1], patch_of(j, 1, b_own, b_left, b_right))
+    for i in range(LEVELS):
+        maps[PC - 1 + i] = finished(lasts[i], table, rows, (i + 1) * PC - 1)
+        write(maps.at[PC - 1 + i], (i + 1) * PC - 1)
     for j in range(PC - 1):
         cross(spec_a.at[j], spec_b.at[j], crossed.at[j])
         turned[j] = dot(table[2], crossed[j]).astype(bf16)
@@ -511,7 +561,8 @@
     results = pl.pallas_call(
         functools.partial(first_kernel, n_sec, n_tile),
         out_shape=(
-            jax.ShapeDtypeStruct((PC + 1, N, N), f32),
+            jax.ShapeDtypeStruct((PC - 1, N, N), f32),
+            held(LEVELS, N, N),
             jax.ShapeDtypeStruct((16, N), f32),
             held(6, N, N),
             jax.ShapeDtypeStruct((PC - 1, N, N), f32),
@@ -520,7 +571,7 @@
             held(LEVELS, EDGE, N),
         ),
         in_specs=[hbm] * 3,
-        out_specs=(vmem,) * 7,
+        out_specs=(vmem,) * 8,
         scratch_shapes=[
             pltpu.VMEM((LEVELS, COLS, N), f32),
             pltpu.VMEM((LEVELS, COLS, N), f32),
@@ -531,6 +582,8 @@
             pltpu.VMEM((4, 8, N), f32),
             pltpu.VMEM((2, 8, N), f32),
             pltpu.VMEM((3, 8, N), f32),
+            columns(COLS),
+            pltpu.VMEM((8, N), f32),
             pltpu.VMEM((PC - 1, N, N), f32),
             pltpu.VMEM((LEVELS, N, N), f32),
             pltpu.VMEM((PC + 1, N, N), f32),
@@ -538,8 +591,8 @@
             pltpu.VMEM((PC + 1, N, N), bf16),
             pltpu.VMEM((16, N), f32),
             pltpu.SemaphoreType.DMA((5,)),
-            pltpu.SemaphoreType.DMA((30,)),
-            pltpu.SemaphoreType.DMA((15,)),
+            pltpu.SemaphoreType.DMA((44,)),
+            pltpu.SemaphoreType.DMA((18,)),
             pltpu.SemaphoreType.REGULAR((2,)),
         ],
         compiler_params=pltpu.CompilerParams(
@@ -550,13 +603,13 @@
     maps = pl.pallas_call(
         last_kernel,
         out_shape=jax.ShapeDtypeStruct((patches, N, N), f32),
-        in_specs=[vmem] * 7,
+        in_specs=[vmem] * 8,
         out_specs=hbm,
         scratch_shapes=[
             pltpu.VMEM((PC - 1, N, N), f32),
             pltpu.VMEM((PC - 1, N, N), bf16),
             pltpu.VMEM((PC - 1, N, N), bf16),
-            pltpu.VMEM((PC - 1, N, N), f32),
+            pltpu.VMEM((PC + 1, N, N), f32),
             pltpu.SemaphoreType.DMA((patches,)),
         ],
         compiler_params=pltpu.CompilerParams(vmem_limit_bytes=16 * 2**20),

time: 16.7 us -> 16.4 us (0.982)
  Pallas kernels: 16.6 us -> 16.3 us
    pallas_call x1, Pallas kernels: 14.9 us -> 14.6 us  [local(): pl.pallas_call(functools.partial(first_kernel, n_sec, n_tile), out_shape=...]
where the time goes in v4:
time: 16.4 us; the launch traced here: 16.3 us
  Pallas kernels  16.3 us (99%)
    pallas_call x1, Pallas kernels, local(): pl.pallas_call(functools.partial(first_kernel, n_sec, n_tile), out_shape=...  14.6 us
    pallas_call x1, Pallas kernels, local(): pl.pallas_call(last_kernel, out_shape=jax.ShapeDtypeStruct((patches, N, N...  1.74 us

profile of v4, /device:TPU:228, one launch (start us, length us, event | category | flops | bytes accessed | tf_op | source)
XLA Modules:
  0.0 16.3 jit_solution(15906983648863706474)
XLA Ops:
  0.0 14.6 %spectra.1 = (f32[3,256,256]{2,1,0:T(8,128)S(1)}, bf16[2,256,256]{2,1,0:T(8,128)(2,1)S(1)}, f32[16,256]{1,0:T(8,128)S(1)}, bf16[6,256,256]{2,1,0:T(8,128)(2,1)S(...) custom-call(f32[2,160,256]{2,1,0:T(8,128)} %bitcast.7, ...), custom_call_target="tpu_custom_call" | custom-call | tf_op jit(solution)/shard_map/spectra/pallas_call | solution.py:561
  14.6 1.7 %maps.1 = f32[8,256,256]{2,1,0:T(8,128)} custom-call(f32[3,256,256]{2,1,0:T(8,128)S(1)} %get-tuple-element.13.held, bf16[2,256,256]{2,1,0:T(8,128)(2,1)S(1)} %get-tuple-element.14.lasts, f32[16,256]{1,0:T(8,128)S(1)} %get-tuple-element.15.rows, bf16[6,256,256]{2,1,0:T(8,128)(2,1)S(1)} %get-tuple-element.16.table, ...), custom_call_target="tpu_custom_call" | custom-call | tf_op jit(solution)/shard_map/maps/pallas_call | solution.py:603

commit v5 on v4

--- a/solution.py
+++ b/solution.py
@@ -189,13 +189,16 @@
     crossing = (s % 2 == 1) & has_next
     left_past = at_middle & crossing
     step = t % middle
+    split, before_split = at_middle & (s != n_sec // 2), before_middle & (s != n_sec // 2)
+    joined = jnp.logical_not(split)
     early = at_middle & (s != n_sec // 2)
     not_early = jnp.logical_not(early)
     far, far_next = s == n_sec // 2 - 1, s == n_sec // 2
     back_out = far & (step >= 1) & (step <= middle // 2)
     back_in = far_next & (step < middle // 2)
-    back_past = far & (step < middle // 2)
+    back_past = far & ((step < middle // 2) | before_middle)
     late_out, late_in = far & before_middle, far_next & before_middle
+    over_out, over_in = far & at_middle, late_in
     relay_out, relay_in = crossing & before_middle, crossing & (t == n_tile - 1)
     edge_out, edge_in = relay_out & jnp.logical_not(far), relay_in & jnp.logical_not(far)
     tile_out, tile_in = relay_out & far, relay_in & far
@@ -223,7 +226,7 @@
             pl.semaphore_signal(barrier, inc=1, device_id=device, device_id_type=MESH)
 
     greet(has_left, to_left)
-    greet(has_right & jnp.logical_not(before_middle), to_right)
+    greet(has_right & jnp.logical_not(before_split), to_right)
     greet(has_prev & jnp.logical_not(late_in), {"sec": s - 1})
     greet(late_out, to_next)
     greet(back_in, {"sec": s - 1, "tile": t + 1})
@@ -231,6 +234,7 @@
     greet(relay_in, {"tile": middle - 1})
     relayed = (first_patches & jnp.logical_not(far_next)) | late_in
     greet(relayed, {"sec": s - 1, "tile": n_tile - 1})
+    greet(over_out, {"sec": s + 1, "tile": t - 1})
 
     @pl.when(s == 0)
     def _():
@@ -314,10 +318,11 @@
 
     def send_columns(i):
         send(tile_out, a_own.at[i, high], b_left.at[i], to_direct, 6 + i)
+        send(tile_out, a_own.at[i], r_own.at[i], to_last, 15 + i)
         right, left = to_sides[i]
         right(not_tile_out)
         send(edge_out, a_own.at[i, high], r_own.at[i, high], to_last, 15 + i)
-        left(elsewhere)
+        left(joined)
         send(back_out, a_own.at[i, low], b_right.at[i], to_back, 8 + i)
 
     to_sides = [columns_to(i) for i in range(LEVELS)]
@@ -334,13 +339,22 @@
     load_first.wait()
     a_own[0] = dot(lowered[0], table[0]).astype(bf16)
 
-    known = [has_left & elsewhere, has_right, has_next & jnp.logical_not(late_out)]
-    known += [relay_out, tile_out, relay_in, back_out, late_in]
+    known = [has_left & joined, has_right, has_next & jnp.logical_not(late_out)]
+    known += [relay_out, tile_out, relay_in, back_out, late_in, over_in]
     pl.semaphore_wait(barrier, sum(v.astype(jnp.int32) for v in known))
 
-    @pl.when(before_middle)
+    @pl.when(before_split)
     def _():
         pl.semaphore_signal(ready_sem.at[1], inc=1, device_id=to_right, device_id_type=MESH)
+
+    @pl.when(over_in)
+    def _():
+        pl.semaphore_signal(
+            ready_sem.at[2],
+            inc=1,
+            device_id={"sec": s - 1, "tile": t + 1},
+            device_id_type=MESH,
+        )
 
     @pl.when(late_in)
     def _():
@@ -352,7 +366,7 @@
     send(tile_out, side_out.at[0], b_side.at[1], to_direct, 13)
     send(edge_out, side_out.at[0], r_side, to_last, 17)
     side_left = prepare(has_left, side_out.at[1], side_in.at[1], to_left, 11)
-    side_left(elsewhere)
+    side_left(joined)
     send(back_out, side_out.at[1], b_side.at[2], to_back, 14)
     send_columns(0)
     a_own[1] = dot(lowered[1], table[0]).astype(bf16)
@@ -360,8 +374,6 @@
     for right, _ in to_sides:
         right(tile_out)
 
-    for i in range(LEVELS):
-        send(tile_out, a_own.at[i], r_own.at[i], to_last, 15 + i)
     send(tile_out, side, r_side, to_last, 17)
     own_on = has_next & not_tile_out
 
@@ -369,22 +381,32 @@
         send(own_on, a_own.at[i], b_own.at[i], to_next, 4 + i)
     send(own_on, side, b_side.at[0], to_next, 12)
 
-    arrived(relay_in, r_side, 17)
-    send(edge_in, r_side, b_side.at[1], to_middle, 13)
-    send(tile_in, r_side, b_side.at[0], to_before, 12)
     for i in range(LEVELS):
         arrived(edge_in, r_own.at[i, high], 15 + i)
         send(edge_in, r_own.at[i, high], b_left.at[i], to_middle, 6 + i)
         arrived(tile_in, r_own.at[i], 15 + i)
         send(tile_in, r_own.at[i], b_own.at[i], to_before, 4 + i)
-
-    @pl.when(at_middle)
+        if i == 0:
+            arrived(edge_in, r_side, 17)
+            send(edge_in, r_side, b_side.at[1], to_middle, 13)
+    arrived(tile_in, r_side, 17)
+    send(tile_in, r_side, b_side.at[0], to_before, 12)
+
+    @pl.when(split)
     def _():
         pl.semaphore_wait(ready_sem.at[1], 1)
 
-    side_left(at_middle)
+    side_left(split)
     for _, left in to_sides:
-        left(at_middle)
+        left(split)
+
+    @pl.when(over_out)
+    def _():
+        pl.semaphore_wait(ready_sem.at[2], 1)
+
+    send(over_out, side_out.at[1], b_side.at[2], to_back, 14)
+    for i in range(LEVELS):
+        send(over_out, a_own.at[i, low], b_right.at[i], to_back, 8 + i)
 
     @pl.when(s == 0)
     def _():
@@ -451,7 +473,7 @@
         for i in levels:
             turned[PC - 1 + i] = dot(table[2], crossed[PC - 1 + i]).astype(bf16)
 
-    upper = step >= middle // 2
+    upper = (step >= middle // 2) & jnp.logical_not(before_middle)
     load_rest.wait()
     pass_right(at_middle, 0)
     pass_right(at_middle, 1)
@@ -591,9 +613,9 @@
             pltpu.VMEM((PC + 1, N, N), bf16),
             pltpu.VMEM((16, N), f32),
             pltpu.SemaphoreType.DMA((5,)),
-            pltpu.SemaphoreType.DMA((44,)),
+            pltpu.SemaphoreType.DMA((47,)),
             pltpu.SemaphoreType.DMA((18,)),
-            pltpu.SemaphoreType.REGULAR((2,)),
+            pltpu.SemaphoreType.REGULAR((3,)),
         ],
         compiler_params=pltpu.CompilerParams(
             collective_id=0, has_side_effects=True, vmem_limit_bytes=16 * 2**20

time: 16.4 us -> 16.2 us (0.988)
  the two profiles are of different devices: /device:TPU:228 before, /device:TPU:102 now
where the time goes in v5:
time: 16.2 us; the launch traced here: 16.1 us
  Pallas kernels  16.1 us (99%)
    pallas_call x1, Pallas kernels, local(): pl.pallas_call(functools.partial(first_kernel, n_sec, n_tile), out_shape=...  14.3 us
    pallas_call x1, Pallas kernels, local(): pl.pallas_call(last_kernel, out_shape=jax.ShapeDtypeStruct((patches, N, N...  1.73 us

profile of v5, /device:TPU:102, one launch (start us, length us, event | category | flops | bytes accessed | tf_op | source)
XLA Modules:
  0.0 16.1 jit_solution(8887517138369440370)
XLA Ops:
  0.0 14.3 %spectra.1 = (f32[3,256,256]{2,1,0:T(8,128)S(1)}, bf16[2,256,256]{2,1,0:T(8,128)(2,1)S(1)}, f32[16,256]{1,0:T(8,128)S(1)}, bf16[6,256,256]{2,1,0:T(8,128)(2,1)S(...) custom-call(f32[2,160,256]{2,1,0:T(8,128)} %bitcast.7, ...), custom_call_target="tpu_custom_call" | custom-call | tf_op jit(solution)/shard_map/spectra/pallas_call | solution.py:583
  14.3 1.7 %maps.1 = f32[8,256,256]{2,1,0:T(8,128)} custom-call(f32[3,256,256]{2,1,0:T(8,128)S(1)} %get-tuple-element.13.held, bf16[2,256,256]{2,1,0:T(8,128)(2,1)S(1)} %get-tuple-element.14.lasts, f32[16,256]{1,0:T(8,128)S(1)} %get-tuple-element.15.rows, bf16[6,256,256]{2,1,0:T(8,128)(2,1)S(1)} %get-tuple-element.16.table, ...), custom_call_target="tpu_custom_call" | custom-call | tf_op jit(solution)/shard_map/maps/pallas_call | solution.py:625

commit v6 on v5

--- a/solution.py
+++ b/solution.py
@@ -317,14 +317,13 @@
         return right, left
 
     def send_columns(i):
+        send(back_out, a_own.at[i, low], b_right.at[i], to_back, 8 + i)
         send(tile_out, a_own.at[i, high], b_left.at[i], to_direct, 6 + i)
         send(tile_out, a_own.at[i], r_own.at[i], to_last, 15 + i)
         right, left = to_sides[i]
         right(not_tile_out)
         send(edge_out, a_own.at[i, high], r_own.at[i, high], to_last, 15 + i)
         left(joined)
-        send(back_out, a_own.at[i, low], b_right.at[i], to_back, 8 + i)
-
     to_sides = [columns_to(i) for i in range(LEVELS)]
     lowered, stats = [], []
     for i in range(LEVELS):
@@ -362,12 +361,12 @@
             ready_sem.at[0], inc=1, device_id={"sec": s - 1}, device_id_type=MESH
         )
 
+    send(back_out, side_out.at[1], b_side.at[2], to_back, 14)
     send(has_right, side_out.at[0], side_in.at[0], to_right, 10)
     send(tile_out, side_out.at[0], b_side.at[1], to_direct, 13)
     send(edge_out, side_out.at[0], r_side, to_last, 17)
     side_left = prepare(has_left, side_out.at[1], side_in.at[1], to_left, 11)
     side_left(joined)
-    send(back_out, side_out.at[1], b_side.at[2], to_back, 14)
     send_columns(0)
     a_own[1] = dot(lowered[1], table[0]).astype(bf16)
     send_columns(1)

time: 16.2 us -> 15.9 us (0.981)
  the two profiles are of different devices: /device:TPU:102 before, /device:TPU:27 now
where the time goes in v6:
time: 15.9 us; the launch traced here: 15.8 us
  Pallas kernels  15.8 us (99%)
    pallas_call x1, Pallas kernels, local(): pl.pallas_call(functools.partial(first_kernel, n_sec, n_tile), out_shape=...  14.1 us
    pallas_call x1, Pallas kernels, local(): pl.pallas_call(last_kernel, out_shape=jax.ShapeDtypeStruct((patches, N, N...  1.74 us

profile of v6, /device:TPU:27, one launch (start us, length us, event | category | flops | bytes accessed | tf_op | source)
XLA Modules:
  0.0 15.8 jit_solution(2367356463561071948)
XLA Ops:
  0.0 14.1 %spectra.1 = (f32[3,256,256]{2,1,0:T(8,128)S(1)}, bf16[2,256,256]{2,1,0:T(8,128)(2,1)S(1)}, f32[16,256]{1,0:T(8,128)S(1)}, bf16[6,256,256]{2,1,0:T(8,128)(2,1)S(...) custom-call(f32[2,160,256]{2,1,0:T(8,128)} %bitcast.7, ...), custom_call_target="tpu_custom_call" | custom-call | tf_op jit(solution)/shard_map/spectra/pallas_call | solution.py:582
  14.1 1.7 %maps.1 = f32[8,256,256]{2,1,0:T(8,128)} custom-call(f32[3,256,256]{2,1,0:T(8,128)S(1)} %get-tuple-element.13.held, bf16[2,256,256]{2,1,0:T(8,128)(2,1)S(1)} %get-tuple-element.14.lasts, f32[16,256]{1,0:T(8,128)S(1)} %get-tuple-element.15.rows, bf16[6,256,256]{2,1,0:T(8,128)(2,1)S(1)} %get-tuple-element.16.table, ...), custom_call_target="tpu_custom_call" | custom-call | tf_op jit(solution)/shard_map/maps/pallas_call | solution.py:624

commit v7 on v6

--- a/solution.py
+++ b/solution.py
@@ -150,7 +150,6 @@
     x_hbm,
     prior_hbm,
     table_hbm,
-    held,
     turned_out,
     rows_out,
     table,
@@ -173,7 +172,6 @@
     spec_last,
     spec_b,
     crossed,
-    turned,
     rows,
     load_sem,
     send_sem,
@@ -470,7 +468,7 @@
         for i in levels:
             cross(spec_last.at[i], spec_b.at[PC - 1 + i], crossed.at[PC - 1 + i])
         for i in levels:
-            turned[PC - 1 + i] = dot(table[2], crossed[PC - 1 + i]).astype(bf16)
+            turned_out[PC - 1 + i] = dot(table[2], crossed[PC - 1 + i]).astype(bf16)
 
     upper = (step >= middle // 2) & jnp.logical_not(before_middle)
     load_rest.wait()
@@ -520,17 +518,13 @@
     for j in range(PC - 1):
         cross(spec_a.at[j], spec_b.at[j], crossed.at[j])
     for j in range(PC - 1):
-        turned[j] = dot(table[2], crossed[j]).astype(bf16)
-    for j in range(PC - 1):
-        held[j] = finished(turned[j], table, rows, j)
+        turned_out[j] = dot(table[2], crossed[j]).astype(bf16)
 
     @pl.when(not_early)
     def _():
         previous_right(1)
         last_patches(0, 1)
 
-    for j in range(LEVELS):
-        turned_out[j] = turned[PC - 1 + j]
     settle(started)
     arrived(has_left, b_left.at[1], 7)
     pl.when(left_on)(passed[1].wait_send)
@@ -544,7 +538,7 @@
 
 
 def last_kernel(
-    held, lasts, rows, table, spec_a, b_own, b_left, b_right, out_hbm, spec_b, crossed, turned, maps, sem
+    before, rows, table, spec_a, b_own, b_left, b_right, out_hbm, spec_b, crossed, turned, maps, sem
 ):
     copies = []
 
@@ -554,18 +548,17 @@
         copies.append(copy)
 
     for j in range(PC - 1):
-        write(held.at[j], j)
-    for j in range(PC - 1):
         spec_b[j] = dot(table[1], patch_of(j, 1, b_own, b_left, b_right))
-    for i in range(LEVELS):
-        maps[PC - 1 + i] = finished(lasts[i], table, rows, (i + 1) * PC - 1)
-        write(maps.at[PC - 1 + i], (i + 1) * PC - 1)
+    for j in range(PC + 1):
+        p = j if j < PC else 2 * PC - 1
+        maps[p] = finished(before[j], table, rows, p)
+        write(maps.at[p], p)
     for j in range(PC - 1):
         cross(spec_a.at[j], spec_b.at[j], crossed.at[j])
         turned[j] = dot(table[2], crossed[j]).astype(bf16)
     for j in range(PC - 1):
-        maps[j] = finished(turned[j], table, rows, PC + j)
-        write(maps.at[j], PC + j)
+        maps[PC + j] = finished(turned[j], table, rows, PC + j)
+        write(maps.at[PC + j], PC + j)
     for copy in copies:
         copy.wait()
 
@@ -582,8 +575,7 @@
     results = pl.pallas_call(
         functools.partial(first_kernel, n_sec, n_tile),
         out_shape=(
-            jax.ShapeDtypeStruct((PC - 1, N, N), f32),
-            held(LEVELS, N, N),
+            held(PC + 1, N, N),
             jax.ShapeDtypeStruct((16, N), f32),
             held(6, N, N),
             jax.ShapeDtypeStruct((PC - 1, N, N), f32),
@@ -592,7 +584,7 @@
             held(LEVELS, EDGE, N),
         ),
         in_specs=[hbm] * 3,
-        out_specs=(vmem,) * 8,
+        out_specs=(vmem,) * 7,
         scratch_shapes=[
             pltpu.VMEM((LEVELS, COLS, N), f32),
             pltpu.VMEM((LEVELS, COLS, N), f32),
@@ -609,7 +601,6 @@
             pltpu.VMEM((LEVELS, N, N), f32),
             pltpu.VMEM((PC + 1, N, N), f32),
             pltpu.VMEM((PC + 1, N, N), bf16),
-            pltpu.VMEM((PC + 1, N, N), bf16),
             pltpu.VMEM((16, N), f32),
             pltpu.SemaphoreType.DMA((5,)),
             pltpu.SemaphoreType.DMA((47,)),
@@ -624,13 +615,13 @@
     maps = pl.pallas_call(
         last_kernel,
         out_shape=jax.ShapeDtypeStruct((patches, N, N), f32),
-        in_specs=[vmem] * 8,
+        in_specs=[vmem] * 7,
         out_specs=hbm,
         scratch_shapes=[
             pltpu.VMEM((PC - 1, N, N), f32),
             pltpu.VMEM((PC - 1, N, N), bf16),
             pltpu.VMEM((PC - 1, N, N), bf16),
-            pltpu.VMEM((PC + 1, N, N), f32),
+            pltpu.VMEM((patches, N, N), f32),
             pltpu.SemaphoreType.DMA((patches,)),
         ],
         compiler_params=pltpu.CompilerParams(vmem_limit_bytes=16 * 2**20),

time: 15.9 us -> 15.8 us (level)
  the two profiles are of different devices: /device:TPU:27 before, /device:TPU:102 now
where the time goes in v7:
time: 15.8 us; the launch traced here: 15.6 us
  Pallas kernels  15.6 us (99%)
    pallas_call x1, Pallas kernels, local(): pl.pallas_call(functools.partial(first_kernel, n_sec, n_tile), out_shape=...  13.7 us
    pallas_call x1, Pallas kernels, local(): pl.pallas_call(last_kernel, out_shape=jax.ShapeDtypeStruct((patches, N, N...  1.88 us

profile of v7, /device:TPU:102, one launch (start us, length us, event | category | flops | bytes accessed | tf_op | source)
XLA Modules:
  0.0 15.6 jit_solution(3103062798823254728)
XLA Ops:
  0.0 13.7 %spectra.1 = (bf16[5,256,256]{2,1,0:T(8,128)(2,1)S(1)}, f32[16,256]{1,0:T(8,128)S(1)}, bf16[6,256,256]{2,1,0:T(8,128)(2,1)S(1)}, f32[3,256,256]{2,1,0:T(8,128)S(...) custom-call(f32[2,160,256]{2,1,0:T(8,128)} %bitcast.7, ...), custom_call_target="tpu_custom_call" | custom-call | tf_op jit(solution)/shard_map/spectra/pallas_call | solution.py:575
  13.7 1.9 %maps.1 = f32[8,256,256]{2,1,0:T(8,128)} custom-call(bf16[5,256,256]{2,1,0:T(8,128)(2,1)S(1)} %get-tuple-element.12.before, f32[16,256]{1,0:T(8,128)S(1)} %get-tuple-element.13.rows, bf16[6,256,256]{2,1,0:T(8,128)(2,1)S(1)} %get-tuple-element.14.table, f32[3,256,256]{2,1,0:T(8,128)S(1)} %get-tuple-element.15.spec_a, ...), custom_call_target="tpu_custom_call" | custom-call | tf_op jit(solution)/shard_map/maps/pallas_call | solution.py:615

commit v8 on v7

--- a/solution.py
+++ b/solution.py
@@ -397,14 +397,6 @@
     for _, left in to_sides:
         left(split)
 
-    @pl.when(over_out)
-    def _():
-        pl.semaphore_wait(ready_sem.at[2], 1)
-
-    send(over_out, side_out.at[1], b_side.at[2], to_back, 14)
-    for i in range(LEVELS):
-        send(over_out, a_own.at[i, low], b_right.at[i], to_back, 8 + i)
-
     @pl.when(s == 0)
     def _():
         load_prior.wait()
@@ -481,6 +473,14 @@
         previous_right(0)
         previous_right(1)
         last_patches(0, 1)
+
+    @pl.when(over_out)
+    def _():
+        pl.semaphore_wait(ready_sem.at[2], 1)
+
+    send(over_out, side_out.at[1], b_side.at[2], to_back, 14)
+    for i in range(LEVELS):
+        send(over_out, a_own.at[i, low], b_right.at[i], to_back, 8 + i)
 
     pass_on(True, has_left, left_on, side_in.at[0], 10, b_side.at[1], 13)
     pass_right_side(upper)

time: 15.8 us -> 15.8 us (level)
  no operation moved by 1% of the time
where the time goes in v8:
time: 15.8 us; the launch traced here: 15.6 us
  Pallas kernels  15.6 us (99%)
    pallas_call x1, Pallas kernels, local(): pl.pallas_call(functools.partial(first_kernel, n_sec, n_tile), out_shape=...  13.7 us
    pallas_call x1, Pallas kernels, local(): pl.pallas_call(last_kernel, out_shape=jax.ShapeDtypeStruct((patches, N, N...  1.88 us

profile of v8, /device:TPU:102, one launch (start us, length us, event | category | flops | bytes accessed | tf_op | source)
XLA Modules:
  0.0 15.6 jit_solution(5708837941899551236)
XLA Ops:
  0.0 13.7 %spectra.1 = (bf16[5,256,256]{2,1,0:T(8,128)(2,1)S(1)}, f32[16,256]{1,0:T(8,128)S(1)}, bf16[6,256,256]{2,1,0:T(8,128)(2,1)S(1)}, f32[3,256,256]{2,1,0:T(8,128)S(...) custom-call(f32[2,160,256]{2,1,0:T(8,128)} %bitcast.7, ...), custom_call_target="tpu_custom_call" | custom-call | tf_op jit(solution)/shard_map/spectra/pallas_call | solution.py:575
  13.7 1.9 %maps.1 = f32[8,256,256]{2,1,0:T(8,128)} custom-call(bf16[5,256,256]{2,1,0:T(8,128)(2,1)S(1)} %get-tuple-element.12.before, f32[16,256]{1,0:T(8,128)S(1)} %get-tuple-element.13.rows, bf16[6,256,256]{2,1,0:T(8,128)(2,1)S(1)} %get-tuple-element.14.table, f32[3,256,256]{2,1,0:T(8,128)S(1)} %get-tuple-element.15.spec_a, ...), custom_call_target="tpu_custom_call" | custom-call | tf_op jit(solution)/shard_map/maps/pallas_call | solution.py:615

commit v9 on v8

--- a/solution.py
+++ b/solution.py
@@ -321,7 +321,7 @@
         right, left = to_sides[i]
         right(not_tile_out)
         send(edge_out, a_own.at[i, high], r_own.at[i, high], to_last, 15 + i)
-        left(joined)
+        left(joined & jnp.logical_not(before_middle))
     to_sides = [columns_to(i) for i in range(LEVELS)]
     lowered, stats = [], []
     for i in range(LEVELS):
@@ -370,6 +370,8 @@
     send_columns(1)
     for right, _ in to_sides:
         right(tile_out)
+    for _, left in to_sides:
+        left(before_middle)
 
     send(tile_out, side, r_side, to_last, 17)
     own_on = has_next & not_tile_out

time: 15.8 us -> 15.8 us (level)
  no operation moved by 1% of the time
where the time goes in v9:
time: 15.8 us; the launch traced here: 15.6 us
  Pallas kernels  15.6 us (99%)
    pallas_call x1, Pallas kernels, local(): pl.pallas_call(functools.partial(first_kernel, n_sec, n_tile), out_shape=...  13.7 us
    pallas_call x1, Pallas kernels, local(): pl.pallas_call(last_kernel, out_shape=jax.ShapeDtypeStruct((patches, N, N...  1.88 us

profile of v9, /device:TPU:102, one launch (start us, length us, event | category | flops | bytes accessed | tf_op | source)
XLA Modules:
  0.0 15.6 jit_solution(4382865941195961114)
XLA Ops:
  0.0 13.7 %spectra.1 = (bf16[5,256,256]{2,1,0:T(8,128)(2,1)S(1)}, f32[16,256]{1,0:T(8,128)S(1)}, bf16[6,256,256]{2,1,0:T(8,128)(2,1)S(1)}, f32[3,256,256]{2,1,0:T(8,128)S(...) custom-call(f32[2,160,256]{2,1,0:T(8,128)} %bitcast.7, ...), custom_call_target="tpu_custom_call" | custom-call | tf_op jit(solution)/shard_map/spectra/pallas_call | solution.py:577
  13.7 1.9 %maps.1 = f32[8,256,256]{2,1,0:T(8,128)} custom-call(bf16[5,256,256]{2,1,0:T(8,128)(2,1)S(1)} %get-tuple-element.12.before, f32[16,256]{1,0:T(8,128)S(1)} %get-tuple-element.13.rows, bf16[6,256,256]{2,1,0:T(8,128)(2,1)S(1)} %get-tuple-element.14.table, f32[3,256,256]{2,1,0:T(8,128)S(1)} %get-tuple-element.15.spec_a, ...), custom_call_target="tpu_custom_call" | custom-call | tf_op jit(solution)/shard_map/maps/pallas_call | solution.py:617
